TPU v7x, 512 devices: a whole 4x8x8 slice. The times are simulated.
512 devices in a mesh: row: 8 (over y), col: 16 (over z, core), rep: 4 (over x).
Axes of the slice: x: 4, y: 8, z: 8, core: 2. Of those that a mesh axis runs over, the one named last changes fastest.
Arguments:
- a_blocks: bfloat16 [128, 128, 64, 128], P('row', ('col', 'rep')), may hold values from -0.0014648438 to 0.0014648438
- a_pattern: int32 [128, 128], P('row', ('col', 'rep')), may hold values 0 or 1
- p_blocks: bfloat16 [128, 32, 64, 128], P('row', 'col'), may hold values from -6 to 6
- p_pattern: int32 [128, 32], P('row', 'col'), may hold values 0 or 1
Outputs:
- coarse: float32 [32, 32, 64, 128], P(('row', 'rep'), 'col')
All inputs are finite; a program needn't handle non-finite values. No bound on the sum of `a_pattern` or of `p_pattern` on one device may be relied on, other than what follows from the above.
Results may differ from a plain program's by a relative error of at most 0.0029.
Values may be sent and summed in bfloat16 or wider, within the bound.
No kernel may reach another device: no remote copies, remote signals or barrier semaphores. Data moves between devices by JAX's collectives and lax.ppermute only.
A program may use at most 64 MiB of HBM per device.

v0:
```python
import jax
import jax.numpy as jnp
from jax import lax
from jax.sharding import PartitionSpec as P


def real_form(blocks):
    half = blocks.shape[-1] // 2
    lower = jnp.concatenate([-blocks[..., half:], blocks[..., :half]], axis=-1)
    return jnp.concatenate([blocks, lower], axis=-2)


def transposed(blocks):
    order = blocks.shape[-2]
    lead = blocks.shape[:-2]
    split = blocks.reshape(lead + (order, 2, order))
    moved = jnp.swapaxes(split, -3, -1)
    return moved.reshape(lead + (order, 2 * order))


def panel_product(right_panel, piece):
    return jnp.einsum(
        "ikxp,kjpq->ijxq", piece, real_form(right_panel), preferred_element_type=jnp.float32
    )


def per_device(a_blocks, a_pattern, p_blocks, p_pattern):
    a_live = jnp.where(a_pattern[:, :, None, None] > 0, a_blocks, jnp.zeros_like(a_blocks))
    p_live = jnp.where(p_pattern[:, :, None, None] > 0, p_blocks, jnp.zeros_like(p_blocks))
    layers = lax.axis_size("rep")
    layer = lax.axis_index("rep")
    rows = a_live.shape[0]
    share = rows // layers
    mine = lax.all_to_all(a_live, "rep", split_axis=0, concat_axis=1, tiled=True)
    panel = lax.all_gather(p_live, "row", axis=0, tiled=True)
    product_rows = panel_product(panel, lax.all_gather(mine, "col", axis=1, tiled=True))
    product = product_rows.astype(jnp.bfloat16)
    right = real_form(product)
    own_rows = lax.dynamic_slice_in_dim(p_live, layer * share, share, 0)
    terms = jnp.einsum(
        "iaxp,ibpq->abxq",
        transposed(lax.all_gather(own_rows, "col", axis=1, tiled=True)),
        right,
        preferred_element_type=jnp.float32,
    )
    return lax.psum_scatter(terms, ("row", "rep"), scatter_dimension=0, tiled=True)


def solution(mesh):
    return jax.shard_map(
        per_device,
        mesh=mesh,
        in_specs=(
            P("row", ("col", "rep"), None, None),
            P("row", ("col", "rep")),
            P("row", "col", None, None),
            P("row", "col"),
        ),
        out_specs=P(("row", "rep"), "col", None, None),
        check_vma=False,
    )
```

profile of v0, /device:TPU:1, one launch (start us, length us, event | category | flops | bytes accessed | tf_op | source)
XLA Modules:
  0.0 357.0 jit_solution(9539983402239409331)
XLA Ops:
  6.5 0.7 broadcast_compare_fusion.1
  7.2 1.1 copy_select_fusion.1
  8.4 0.7 constant_dynamic-slice_fusion
  9.1 0.0 all-gather.4.cloned.1.call-start
  9.2 0.0 copy-done
  9.2 0.7 all-gather.4.cloned.1.call-update
  9.9 0.7 broadcast_compare_fusion
  10.6 1.1 copy_select_fusion
  11.8 11.6 %all_to_all.18 = bf16[16,2,64,128]{3,2,1,0:T(8,128)(2,1)S(1)} all-to-all(bf16[16,2,64,128]{3,2,1,0:T(8,128)(2,1)S(1)} %copy.12), channel_id=1, replica_groups=mesh['row'=8,'col'=16,'rep'=4] {'rep'}, dimensions={0} | all-to-all | bytes 1048576 | tf_op jit(solution)/shard_map/all_to_all | solution.py:34
  23.4 0.8 copy.13
  24.3 0.0 all-reduce.3.cloned.1.call-start
  24.3 34.3 %all-gather.8.cloned.1.call-done = bf16[4,32,64,128]{3,2,0,1:T(8,128)(2,1)} async-done(((bf16[4,2,64,128]{3,2,0,1:T(8,128)(2,1)}), bf16[4,32,64,128]{3,2,0,1:T(8,128)(2,1)}) %all-gather.8.cloned.1.call-update) | async-done | bytes 2097168 | tf_op jit(solution)/shard_map/all_gather | solution.py:42
  58.6 8.2 %reshape.10 = bf16[4,32,64,2,64]{4,3,2,0,1:T(2,128)(2,1)} reshape(bf16[4,32,64,128]{3,2,0,1:T(8,128)(2,1)} %all-gather.8.cloned.1.call-done) | data formatting | bytes 4194304 | tf_op jit(solution)/shard_map/reshape | solution.py:16
  66.8 15.0 %copy.14 = bf16[4,32,64,2,64]{2,3,4,0,1:T(2,128)(2,1)} copy(bf16[4,32,64,2,64]{4,3,2,0,1:T(2,128)(2,1)} %reshape.10) | data formatting | bytes 4194304 | tf_op jit(solution)/shard_map/reshape | solution.py:16
  81.8 6.8 %reshape.16 = bf16[4,32,64,128,1]{3,2,0,1,4:T(8,128)(2,1)S(1)} reshape(bf16[4,32,64,2,64]{4,3,2,0,1:T(2,128)(2,1)} %bitcast.60) | data formatting | bytes 4194304 | tf_op jit(solution)/shard_map/reshape | solution.py:18
  88.6 26.9 %all-gather.4.cloned.1.call-done = bf16[128,2,64,128]{3,2,0,1:T(8,128)(2,1)} async-done(((bf16[16,2,64,128]{3,2,0,1:T(8,128)(2,1)}), bf16[128,2,64,128]{3,2,0,1:T(8,128)(2,1)}) %all-gather.4.cloned.1.call-update) | async-done | bytes 4194320 | tf_op jit(solution)/shard_map/all_gather | solution.py:35
  115.5 7.5 %slice_negate_fusion = (bf16[128,2,64,64]{3,2,0,1:T(8,128)(2,1)}, bf16[128,2,64,64]{3,2,0,1:T(8,128)(2,1)}) fusion(bf16[128,2,64,128]{3,2,0,1:T(8,128)(2,1)} %all-gather.4.cloned.1.call-done), kind=kLoop, calls=%fused_computation.7 | loop fusion | flops 1048576 | bytes 8388608 | tf_op jit(solution)/shard_map/neg | solution.py:9
  123.0 53.5 %all-gather.6.cloned.1.call-done = bf16[4,128,64,128]{3,2,1,0:T(8,128)(2,1)} async-done(((bf16[4,8,64,128]{3,2,1,0:T(8,128)(2,1)}), bf16[4,128,64,128]{3,2,1,0:T(8,128)(2,1)}) %all-gather.6.cloned.1.call-update) | async-done | bytes 8388624 | tf_op jit(solution)/shard_map/all_gather | solution.py:36
  176.5 10.4 %fusion.12 = bf16[4,2,64,128]{3,2,0,1:T(8,128)(2,1)S(1)} fusion(bf16[4,128,64,128]{3,2,1,0:T(8,128)(2,1)} %all-gather.6.cloned.1.call-done, bf16[128,2,64,64]{3,2,0,1:T(8,128)(2,1)} %get-tuple-element.6, bf16[128,2,64,64]{3,2,0,1:T(8,128)(2,1)} %get-tuple-element.5, bf16[128,2,64,128]{3,2,0,1:T(8,128)(2,1)} %all-gather.4.cloned.1.call-done), kind=kOutput, calls=%fused_computation.11 | convolution fusion | flops 2172715008 | bytes 16908288 | tf_op jit(solution)/shard_map/ikxp,kjpq->ijxq/dot_general | solution.py:22
  186.9 0.1 slice_negate_fusion.1
  187.0 2.1 convolution_bitcast_fusion
  189.1 1.4 dynamic-slice
  190.5 157.8 %all-reduce.3.cloned.1.call-done = f32[32,2,64,128]{3,2,0,1:T(8,128)} async-done(((f32[32,2,64,128]{3,2,0,1:T(8,128)}), f32[32,2,64,128]{3,2,0,1:T(8,128)}) %all-reduce.3.cloned.1.call-update) | async-done | bytes 2097168
  348.3 2.2 dynamic-slice_bitcast_fusion
  (7 shorter events, 0.1 us)
Async XLA Ops:
  6.5 52.1 %all-gather.8.cloned.1.call-start = ((), (), s32[]{:S(2)}) async-start(), calls=%async_computation.3 | async-start | bytes 2228224 | tf_op jit(solution)/shard_map/all_gather | solution.py:42
  8.4 0.8 copy-start
  9.1 106.4 %all-gather.4.cloned.1.call-start = ((), (), s32[]{:S(2)}) async-start(), calls=%async_computation.1 | async-start | bytes 4718592 | tf_op jit(solution)/shard_map/all_gather | solution.py:35
  9.9 166.6 %all-gather.6.cloned.1.call-start = ((), (), s32[]{:S(2)}) async-start(), calls=%async_computation.2 | async-start | bytes 8912896 | tf_op jit(solution)/shard_map/all_gather | solution.py:36
  24.3 324.0 %all-reduce.3.cloned.1.call-start = ((), (), s32[]{:S(2)}) async-start(), calls=%async_computation.4 | async-start | bytes 4194304
Sparse Core Ops, SparseCore 0:
  9.5 49.0 all-gather.7
  60.7 54.7 all-gather.3
  117.7 58.7 all-gather.5
  189.2 158.9 all-reduce.2
where the time goes:
time: 360 us; the launch traced here: 357 us
  waiting for transfers between devices  273 us (76%)
  local copies, waits for them, and re-layouts  35.2 us (10%)
  between operations  13.2 us (4%)
  matrix products  12.5 us (3%)
  blocking collectives  11.6 us (3%)
  other arithmetic  11.3 us (3%)
    unnamed x5, waiting for transfers between devices  158 us
    all_gather x1, waiting for transfers between devices, per_device(): lax.all_gather(mine, 'col', axis=1, tiled=True)  53.5 us
    all_gather x1, waiting for transfers between devices, per_device(): lax.all_gather(own_rows, 'col', axis=1, tiled=True)  34.3 us
    all_gather x1, waiting for transfers between devices, per_device(): panel = lax.all_gather(p_live, 'row', axis=0, tiled=True)  26.9 us
    reshape x2, local copies, waits for them, and re-layouts, transposed(): split = blocks.reshape(lead + (order, 2, order))  23.2 us
    all_to_all x1, blocking collectives, per_device(): lax.all_to_all(a_live, 'rep', split_axis=0, concat_axis=1, tiled=True)  11.6 us
    dot_general x1, matrix products, panel_product(): jnp.einsum('ikxp,kjpq->ijxq', piece, real_form(right_panel), preferred_el...  10.4 us
    neg x2, other arithmetic, real_form(): lower = jnp.concatenate([-blocks[..., half:], blocks[..., :half]], axis=-1)  7.61 us
  transfers between devices with their start and end apart: 4, of which 4 were waited for; matrix products, arithmetic and copies ran while one was open for 12% of the time, Pallas kernels for 0%

commit v1 on v0

v1 whole, which is shorter than its diff:
```python
import functools

import jax
import jax.numpy as jnp
from jax import lax
from jax.experimental import pallas as pl
from jax.experimental.pallas import tpu as pltpu
from jax.sharding import Mesh, PartitionSpec as P

BLOCK = 64
BF16 = jnp.bfloat16
F32 = jnp.float32


def lower_half(block):
    lane = lax.broadcasted_iota(jnp.int32, block.shape, block.ndim - 1)
    turned = jnp.concatenate([block[..., BLOCK:], block[..., :BLOCK]], axis=-1)
    return jnp.where(lane < BLOCK, -turned, turned)


def real_pair(blocks):
    return jnp.concatenate([jnp.concatenate([b, lower_half(b)], axis=0) for b in blocks], axis=1)


def product_kernel(a_ref, p_ref, out_ref):
    step = pl.program_id(0)
    rows = a_ref.shape[1]
    left = jnp.concatenate(
        [a_ref[0, :, e].reshape(rows * BLOCK, 2 * BLOCK) for e in range(2)], axis=1
    )
    right = jnp.concatenate([real_pair([p_ref[0, e, 0], p_ref[0, e, 1]]) for e in range(2)], axis=0)
    term = jnp.dot(left, right, preferred_element_type=F32)
    for b in range(2):
        part = term[:, b * 2 * BLOCK : (b + 1) * 2 * BLOCK].reshape(rows, BLOCK, 2 * BLOCK)

        @pl.when(step == 0)
        def _():
            out_ref[:, b] = part

        @pl.when(step > 0)
        def _():
            out_ref[:, b] += part


def partial_product(a_all, p_all):
    steps, rows = a_all.shape[0], a_all.shape[1]
    return pl.pallas_call(
        product_kernel,
        grid=(steps,),
        in_specs=[
            pl.BlockSpec((1, rows, 2, BLOCK, 2 * BLOCK), lambda s: (s, 0, 0, 0, 0)),
            pl.BlockSpec((1, 2, 2, BLOCK, 2 * BLOCK), lambda s: (s, 0, 0, 0, 0)),
        ],
        out_specs=pl.BlockSpec((rows, 2, BLOCK, 2 * BLOCK), lambda s: (0, 0, 0, 0)),
        out_shape=jax.ShapeDtypeStruct((rows, 2, BLOCK, 2 * BLOCK), F32),
        name="product_terms",
    )(a_all, p_all)


def sum_kernel(copies, in_ref, out_ref):
    total = in_ref[0]
    for s in range(1, in_ref.shape[0]):
        total = total + in_ref[s]
    rounded = total.astype(BF16)
    for c in range(copies):
        out_ref[c] = rounded


def coarse_kernel(left_ref, prod_ref, out_ref):
    groups = left_ref.shape[0]
    total = jnp.zeros((groups * BLOCK, 4 * BLOCK), F32)
    for i in range(0, prod_ref.shape[0], 2):
        left = jnp.concatenate(
            [
                left_ref[:, (i + e) // 8, (i + e) % 8].reshape(groups * BLOCK, 2 * BLOCK)
                for e in range(2)
            ],
            axis=1,
        )
        right = jnp.concatenate(
            [real_pair([prod_ref[i + e, 0], prod_ref[i + e, 1]]) for e in range(2)], axis=0
        )
        total = total + jnp.dot(left, right, preferred_element_type=F32)
    for b in range(2):
        out_ref[:, b] = (
            total[:, b * 2 * BLOCK : (b + 1) * 2 * BLOCK]
            .reshape(groups, BLOCK, 2 * BLOCK)
            .astype(BF16)
        )


def final_kernel(in_ref, out_ref):
    total = in_ref[0].astype(F32)
    for s in range(1, in_ref.shape[0]):
        total = total + in_ref[s].astype(F32)
    out_ref[0] = total


def call(kernel, out_shape, *args):
    return pl.pallas_call(
        kernel,
        out_shape=out_shape,
        in_specs=[pl.BlockSpec(memory_space=pltpu.VMEM)] * len(args),
        out_specs=pl.BlockSpec(memory_space=pltpu.VMEM),
        compiler_params=pltpu.CompilerParams(vmem_limit_bytes=32 * 1024 * 1024),
    )(*args)


def transposed(blocks):
    lead = blocks.shape[:-2]
    split = blocks.reshape(lead + (BLOCK, 2, BLOCK))
    return jnp.swapaxes(split, -3, -1).reshape(lead + (BLOCK, 2 * BLOCK))


def per_device(a_blocks, a_pattern, p_blocks, p_pattern):
    x = lax.axis_index("rep")
    core = lax.axis_index("core")
    layers, rings = lax.axis_size("rep"), lax.axis_size("row")
    a_live = jnp.where(a_pattern[:, :, None, None] > 0, a_blocks, jnp.zeros_like(a_blocks))
    a_all = lax.all_gather(a_live, ("z", "core"), axis=0, tiled=False)
    p_live = jnp.where(p_pattern[:, :, None, None] > 0, p_blocks, jnp.zeros_like(p_blocks))

    mine = lax.dynamic_slice_in_dim(
        p_live.reshape(2, 4, 2, 2, BLOCK, 2 * BLOCK), x, 1, axis=1
    ).reshape(1, 2, 2, 2, BLOCK, 2 * BLOCK)
    met = lax.all_to_all(
        jnp.broadcast_to(mine, (rings,) + mine.shape[1:]), "row", 0, 0, tiled=True
    )

    column = lax.dynamic_index_in_dim(p_live, x % 2, axis=1, keepdims=False)
    column = transposed(column).reshape(2, 8, BLOCK, 2 * BLOCK)
    own = lax.dynamic_index_in_dim(column, core, axis=0, keepdims=False)
    other = lax.dynamic_index_in_dim(column, 1 - core, axis=0, keepdims=False)
    got = lax.ppermute(other, "core", [(0, 1), (1, 0)])
    left = lax.all_gather(
        jnp.where(core == x // 2, own, got), ("z", "core"), axis=0, tiled=False
    ).reshape(8, 2, 8, BLOCK, 2 * BLOCK)

    terms = partial_product(a_all, met.reshape(2 * rings, 2, 2, BLOCK, 2 * BLOCK))
    swapped = lax.all_to_all(terms, "rep", 0, 0, tiled=True)
    share = terms.shape[0] // layers
    product = call(
        functools.partial(sum_kernel, layers),
        jax.ShapeDtypeStruct((layers, share, 2, BLOCK, 2 * BLOCK), BF16),
        swapped.reshape(layers, share, 2, BLOCK, 2 * BLOCK),
    )
    product = lax.all_to_all(product, "rep", 0, 0, tiled=True)
    coarse = call(
        coarse_kernel,
        jax.ShapeDtypeStruct((8, 2, BLOCK, 2 * BLOCK), BF16),
        left,
        product.reshape(layers * share, 2, BLOCK, 2 * BLOCK),
    )
    coarse = lax.all_to_all(coarse, "row", 0, 0, tiled=True)
    return call(final_kernel, jax.ShapeDtypeStruct((1, 2, BLOCK, 2 * BLOCK), F32), coarse)


def solution(mesh):
    rows, cols, reps = (mesh.shape[name] for name in ("row", "col", "rep"))
    fine = Mesh(mesh.devices.reshape(rows, cols // 2, 2, reps), ("row", "z", "core", "rep"))
    return jax.shard_map(
        per_device,
        mesh=fine,
        in_specs=(
            P("row", ("z", "core", "rep"), None, None),
            P("row", ("z", "core", "rep")),
            P("row", ("z", "core"), None, None),
            P("row", ("z", "core")),
        ),
        out_specs=P(("row", "rep"), ("z", "core"), None, None),
        check_vma=False,
    )
```

time: 360 us -> 147 us (0.41)
  waiting for transfers between devices: 273 us -> 27.3 us
  blocking collectives: 11.6 us -> 66.6 us
  local copies, waits for them, and re-layouts: 35.2 us -> 4.57 us
  Pallas kernels: 0 us -> 16.2 us
  matrix products: 12.5 us -> 0 us
  starting transfers between devices: 0.12 us -> 12.3 us
  other arithmetic: 11.3 us -> 4.45 us
    unnamed x5 -> x2, waiting for transfers between devices: 158 us -> 0.03 us
    all_gather x3 -> x2, waiting for transfers between devices: 115 us -> 25.1 us  [the longest x1 18.5 us: per_device(): a_all = lax.all_gather(a_live, ('z', 'core'), axis=0, tiled=False)]
    all_to_all x1 -> x3, blocking collectives: 11.6 us -> 66.6 us  [the longest x1 32.3 us: per_device(): lax.all_to_all(jnp.broadcast_to(mine, (rings,) + mine.shape[1:]), 'row',...]
    reshape x3 -> x1, local copies, waits for them, and re-layouts: 30 us -> 0.24 us  [transposed(): split = blocks.reshape(lead + (BLOCK, 2, BLOCK))]
    pallas_call x0 -> x4, Pallas kernels: none -> 16.2 us  [the longest x1 13.9 us: partial_product(): pl.pallas_call(product_kernel, grid=(steps,), in_specs=[pl.BlockSpec((1,...]
    dot_general x2 -> x0, matrix products: 12.5 us -> none  [the longest x1 10.4 us: panel_product(): jnp.einsum('ikxp,kjpq->ijxq', piece, real_form(right_panel), preferred_el...]
    ppermute x0 -> x1, starting transfers between devices: none -> 8.79 us  [per_device(): got = lax.ppermute(other, 'core', [(0, 1), (1, 0)])]
    neg x2 -> x0, other arithmetic: 7.61 us -> none  [real_form(): lower = jnp.concatenate([-blocks[..., half:], blocks[..., :half]], axis=-1)]
  transfers between devices with their start and end apart: 4 -> 4, of which waited for: 4 -> 4; matrix products, arithmetic and copies ran while one was open for 12% -> 3% of each run, Pallas kernels for 0% -> 10%
where the time goes in v1:
time: 147 us; the launch traced here: 145 us
  blocking collectives  66.6 us (45%)
  waiting for transfers between devices  27.3 us (19%)
  Pallas kernels  16.2 us (11%)
  between operations  13.5 us (9%)
  starting transfers between devices  12.3 us (8%)
  local copies, waits for them, and re-layouts  4.57 us (3%)
  other arithmetic  4.45 us (3%)
    all_to_all x1, blocking collectives, per_device(): lax.all_to_all(jnp.broadcast_to(mine, (rings,) + mine.shape[1:]), 'row',...  32.3 us
    all_to_all x1, blocking collectives, per_device(): swapped = lax.all_to_all(terms, 'rep', 0, 0, tiled=True)  18.6 us
    all_gather x1, waiting for transfers between devices, per_device(): a_all = lax.all_gather(a_live, ('z', 'core'), axis=0, tiled=False)  18.5 us
    all_to_all x1, blocking collectives, per_device(): coarse = lax.all_to_all(coarse, 'row', 0, 0, tiled=True)  15.7 us
    pallas_call x1, Pallas kernels, partial_product(): pl.pallas_call(product_kernel, grid=(steps,), in_specs=[pl.BlockSpec((1,...  13.9 us
    ppermute x1, starting transfers between devices, per_device(): got = lax.ppermute(other, 'core', [(0, 1), (1, 0)])  8.79 us
    all_gather x1, waiting for transfers between devices, per_device(): lax.all_gather(jnp.where(core == x // 2, own, got), ('z', 'core'), axis=0...  6.56 us
    all_to_all x1, starting transfers between devices, per_device(): product = lax.all_to_all(product, 'rep', 0, 0, tiled=True)  3.47 us
  transfers between devices with their start and end apart: 4, of which 4 were waited for; matrix products, arithmetic and copies ran while one was open for 3% of the time, Pallas kernels for 10%

profile of v1, /device:TPU:1, one launch (start us, length us, event | category | flops | bytes accessed | tf_op | source)
XLA Modules:
  0.0 145.0 jit_solution(16711949728575678079)
XLA Ops:
  6.5 0.7 broadcast_compare_fusion
  7.2 0.1 copy.14
  7.3 1.9 %broadcast_select_fusion = bf16[16,2,64,128]{3,2,1,0:T(8,128)(2,1)} fusion(bf16[16,2,64,128]{3,2,1,0:T(8,128)(2,1)} %param.4, pred[16,2]{1,0:T(8,128)(4,1)S(1)} %copy.14), kind=kLoop, calls=%fused_computation | loop fusion | flops 262144 | bytes 1048608 | tf_op jit(solution)/shard_map/jit(_where)/select_n | solution.py:119
  9.4 0.1 copy.12
  9.5 1.1 broadcast_select_fusion.1
  10.7 0.2 reshape.25
  10.9 2.0 %copy.13 = bf16[16,64,2,64]{3,2,1,0:T(2,128)(2,1)S(1)} copy(bf16[16,64,2,64]{1,2,3,0:T(2,128)(2,1)S(1)} %bitcast.20) | data formatting | bytes 524288 | tf_op jit(solution)/shard_map/transpose | solution.py:112
  12.9 0.2 reshape_reshape.3
  13.2 8.8 %collective-permute-start = (bf16[8,64,128]{2,1,0:T(8,128)(2,1)S(1)}, bf16[8,64,128]{2,1,0:T(8,128)(2,1)S(1)}, u32[]{:S(2)}, u32[]{:S(2)}) collective-permute-start(bf16[8,64,128]{2,1,0:T(8,128)(2,1)S(1)} %dynamic-slice_bitcast_fusion.1), channel_id=1, source_target_pairs={{0,4},{4,0},{1,5},{5,1},{2,6},{6,2},{3,7},{7,3},{8,12},{12,8},{9,1... | collective-permute-start | bytes 393224 | tf_op jit(solution)/shard_map/ppermute | solution.py:134
  22.0 0.9 collective-permute-done
  22.9 0.7 bitcast_select_fusion
  23.7 0.2 broadcast_in_dim.25
  23.9 32.3 %all_to_all.20 = bf16[8,2,2,2,64,128]{5,4,3,2,1,0:T(8,128)(2,1)} all-to-all(bf16[8,2,2,2,64,128]{5,4,3,2,1,0:T(8,128)(2,1)S(1)} %broadcast_in_dim.25), channel_id=1, replica_groups=mesh['row'=8,'z'=8,'core'=2,'rep'=4] {'row'}, dimensions={0} | all-to-all | bytes 2097152 | tf_op jit(solution)/shard_map/all_to_all | solution.py:126
  56.2 18.5 %all-gather.7.cloned.1.call-done = bf16[256,2,64,128]{3,2,1,0:T(8,128)(2,1)} async-done(((bf16[16,2,64,128]{3,2,1,0:T(8,128)(2,1)}), bf16[256,2,64,128]{3,2,1,0:T(8,128)(2,1)}) %all-gather.7.cloned.1.call-update) | async-done | bytes 8388624 | tf_op jit(solution)/shard_map/all_gather | solution.py:120
  74.8 13.9 %product_terms.1 = f32[16,2,64,128]{3,2,1,0:T(8,128)} custom-call(bf16[16,16,2,64,128]{4,3,2,1,0:T(8,128)(2,1)} %bitcast.18, bf16[16,2,2,64,128]{4,3,2,1,0:T(8,128)(2,1)} %bitcast.19), custom_call_target="tpu_custom_call" | custom-call | tf_op jit(solution)/shard_map/product_terms/pallas_call | solution.py:47
  88.7 18.6 %all_to_all.21 = f32[16,2,64,128]{3,2,1,0:T(8,128)S(1)} all-to-all(f32[16,2,64,128]{3,2,1,0:T(8,128)} %product_terms.1), channel_id=1, replica_groups=mesh['row'=8,'z'=8,'core'=2,'rep'=4] {'rep'}, dimensions={0} | all-to-all | bytes 2097152 | tf_op jit(solution)/shard_map/all_to_all | solution.py:140
  107.3 0.9 shard_map.46
  108.1 3.5 %all-to-all-start.2 = ((bf16[4,4,2,64,128]{4,3,2,1,0:T(8,128)(2,1)}), bf16[4,4,2,64,128]{4,3,2,1,0:T(8,128)(2,1)S(1)}, u32[]{:S(2)}, u32[]{:S(2)}) async-start(bf16[4,4,2,64,128]{4,3,2,1,0:T(8,128)(2,1)} %shard_map.46), calls=%async_computation.2 | async-start | bytes 1048576 | tf_op jit(solution)/shard_map/all_to_all | solution.py:147
  111.6 6.6 %all-gather.5.cloned.1.call-done = bf16[128,64,128]{2,1,0:T(8,128)(2,1)} async-done(((bf16[8,64,128]{2,1,0:T(8,128)(2,1)}), bf16[128,64,128]{2,1,0:T(8,128)(2,1)}) %all-gather.5.cloned.1.call-update) | async-done | bytes 2097168 | tf_op jit(solution)/shard_map/all_gather | solution.py:135
  118.2 1.2 all-to-all-done.2
  119.4 1.6 %copy-done = bf16[128,64,128]{2,1,0:T(8,128)(2,1)S(1)} copy-done((bf16[128,64,128]{2,1,0:T(8,128)(2,1)S(1)}, bf16[128,64,128]{2,1,0:T(8,128)(2,1)}, u32[]{:S(2)}) %copy-start) | copy-done | bytes 2097176
  121.0 0.8 shard_map.47
  121.8 15.7 %all_to_all.22.in_ref = bf16[8,2,64,128]{3,2,1,0:T(8,128)(2,1)S(1)} all-to-all(bf16[8,2,64,128]{3,2,1,0:T(8,128)(2,1)S(1)} %shard_map.47), channel_id=1, replica_groups=mesh['row'=8,'z'=8,'core'=2,'rep'=4] {'row'}, dimensions={0} | all-to-all | bytes 524288 | tf_op jit(solution)/shard_map/all_to_all | solution.py:154
  137.4 0.7 shard_map.48
  (8 shorter events, 0.1 us)
Async XLA Ops:
  6.5 68.2 %all-gather.7.cloned.1.call-start = ((), (), s32[]{:S(2)}) async-start(), calls=%async_computation.5 | async-start | bytes 8912896 | tf_op jit(solution)/shard_map/all_gather | solution.py:120
  9.3 108.9 %all-gather.5.cloned.1.call-start = ((), (), s32[]{:S(2)}) async-start(), calls=%async_computation.4 | async-start | bytes 2228224 | tf_op jit(solution)/shard_map/all_gather | solution.py:135
  13.2 9.8 %collective-permute-start = (bf16[8,64,128]{2,1,0:T(8,128)(2,1)S(1)}, bf16[8,64,128]{2,1,0:T(8,128)(2,1)S(1)}, u32[]{:S(2)}, u32[]{:S(2)}) collective-permute-start(bf16[8,64,128]{2,1,0:T(8,128)(2,1)S(1)} %dynamic-slice_bitcast_fusion.1), channel_id=1, source_target_pairs={{0,4},{4,0},{1,5},{5,1},{2,6},{6,2},{3,7},{7,3},{8,12},{12,8},{9,1... | collective-permute-start | bytes 393224 | tf_op jit(solution)/shard_map/ppermute | solution.py:134
  108.1 11.3 %all-to-all-start.2 = ((bf16[4,4,2,64,128]{4,3,2,1,0:T(8,128)(2,1)}), bf16[4,4,2,64,128]{4,3,2,1,0:T(8,128)(2,1)S(1)}, u32[]{:S(2)}, u32[]{:S(2)}) async-start(bf16[4,4,2,64,128]{4,3,2,1,0:T(8,128)(2,1)} %shard_map.46), calls=%async_computation.2 | async-start | bytes 1048576 | tf_op jit(solution)/shard_map/all_to_all | solution.py:147
  119.4 1.6 %copy-start = (bf16[128,64,128]{2,1,0:T(8,128)(2,1)S(1)}, bf16[128,64,128]{2,1,0:T(8,128)(2,1)}, u32[]{:S(2)}) copy-start(bf16[128,64,128]{2,1,0:T(8,128)(2,1)} %all-gather.5.cloned.1.call-done) | copy-start | bytes 6291460
Sparse Core Ops, SparseCore 0:
  9.5 65.2 all-gather.6
  76.9 41.2 all-gather.4

commit v2 on v1

--- a/solution.py
+++ b/solution.py
@@ -22,39 +22,55 @@
     return jnp.concatenate([jnp.concatenate([b, lower_half(b)], axis=0) for b in blocks], axis=1)
 
 
-def product_kernel(a_ref, p_ref, out_ref):
-    step = pl.program_id(0)
-    rows = a_ref.shape[1]
-    left = jnp.concatenate(
-        [a_ref[0, :, e].reshape(rows * BLOCK, 2 * BLOCK) for e in range(2)], axis=1
-    )
-    right = jnp.concatenate([real_pair([p_ref[0, e, 0], p_ref[0, e, 1]]) for e in range(2)], axis=0)
-    term = jnp.dot(left, right, preferred_element_type=F32)
+def product_kernel(pattern_ref, a_ref, p_ref, out_ref, right):
+    groups, part = a_ref.shape[0], a_ref.shape[1]
+    step, steps = pl.program_id(0), pl.num_programs(0)
+    zero = jnp.zeros((BLOCK, 2 * BLOCK), BF16)
+
+    @pl.when(step == 0)
+    def _():
+        for g in range(groups):
+            right[g] = jnp.concatenate(
+                [real_pair([p_ref[g, e, 0], p_ref[g, e, 1]]) for e in range(2)], axis=0
+            )
+
+    total = jnp.zeros((part * BLOCK, 4 * BLOCK), F32)
+    for g in range(groups):
+        at = (g * steps + step) * part * 2
+        sides = [
+            jnp.concatenate(
+                [
+                    jnp.where(pattern_ref[at + 2 * i + e] > 0, a_ref[g, i, e], zero)
+                    for i in range(part)
+                ],
+                axis=0,
+            )
+            for e in range(2)
+        ]
+        total += jnp.dot(
+            jnp.concatenate(sides, axis=1), right[g], preferred_element_type=F32
+        )
     for b in range(2):
-        part = term[:, b * 2 * BLOCK : (b + 1) * 2 * BLOCK].reshape(rows, BLOCK, 2 * BLOCK)
-
-        @pl.when(step == 0)
-        def _():
-            out_ref[:, b] = part
-
-        @pl.when(step > 0)
-        def _():
-            out_ref[:, b] += part
+        out_ref[:, b] = total[:, b * 2 * BLOCK : (b + 1) * 2 * BLOCK].reshape(part, BLOCK, 2 * BLOCK)
 
 
-def partial_product(a_all, p_all):
-    steps, rows = a_all.shape[0], a_all.shape[1]
+def partial_product(pattern, a_all, p_all, part=8):
+    groups, rows = a_all.shape[0], a_all.shape[1]
+    block = (BLOCK, 2 * BLOCK)
     return pl.pallas_call(
         product_kernel,
-        grid=(steps,),
+        grid=(rows // part,),
         in_specs=[
-            pl.BlockSpec((1, rows, 2, BLOCK, 2 * BLOCK), lambda s: (s, 0, 0, 0, 0)),
-            pl.BlockSpec((1, 2, 2, BLOCK, 2 * BLOCK), lambda s: (s, 0, 0, 0, 0)),
+            pl.BlockSpec(memory_space=pltpu.SMEM),
+            pl.BlockSpec((groups, part, 2) + block, lambda s: (0, s, 0, 0, 0)),
+            pl.BlockSpec((groups, 2, 2) + block, lambda s: (0, 0, 0, 0, 0)),
         ],
-        out_specs=pl.BlockSpec((rows, 2, BLOCK, 2 * BLOCK), lambda s: (0, 0, 0, 0)),
-        out_shape=jax.ShapeDtypeStruct((rows, 2, BLOCK, 2 * BLOCK), F32),
+        out_specs=pl.BlockSpec((part, 2) + block, lambda s: (s, 0, 0, 0)),
+        out_shape=jax.ShapeDtypeStruct((rows, 2) + block, F32),
+        scratch_shapes=[pltpu.VMEM((groups, 4 * BLOCK, 4 * BLOCK), BF16)],
+        compiler_params=pltpu.CompilerParams(vmem_limit_bytes=32 * 1024 * 1024),
         name="product_terms",
-    )(a_all, p_all)
+    )(pattern, a_all, p_all)
 
 
 def sum_kernel(copies, in_ref, out_ref):
@@ -116,8 +132,11 @@
     x = lax.axis_index("rep")
     core = lax.axis_index("core")
     layers, rings = lax.axis_size("rep"), lax.axis_size("row")
-    a_live = jnp.where(a_pattern[:, :, None, None] > 0, a_blocks, jnp.zeros_like(a_blocks))
-    a_all = lax.all_gather(a_live, ("z", "core"), axis=0, tiled=False)
+    a_all = lax.all_gather(a_blocks, ("z", "core"), axis=0, tiled=False)
+    columns = 2 * lax.axis_size("z")
+    kept = lax.all_to_all(
+        jnp.broadcast_to(a_pattern[None], (columns,) + a_pattern.shape), ("z", "core"), 0, 0, tiled=True
+    )
     p_live = jnp.where(p_pattern[:, :, None, None] > 0, p_blocks, jnp.zeros_like(p_blocks))
 
     mine = lax.dynamic_slice_in_dim(
@@ -136,7 +155,7 @@
         jnp.where(core == x // 2, own, got), ("z", "core"), axis=0, tiled=False
     ).reshape(8, 2, 8, BLOCK, 2 * BLOCK)
 
-    terms = partial_product(a_all, met.reshape(2 * rings, 2, 2, BLOCK, 2 * BLOCK))
+    terms = partial_product(kept.reshape(-1), a_all, met.reshape(2 * rings, 2, 2, BLOCK, 2 * BLOCK))
     swapped = lax.all_to_all(terms, "rep", 0, 0, tiled=True)
     share = terms.shape[0] // layers
     product = call(

time: 147 us -> 147 us (level)
  blocking collectives: 66.6 us -> 36.5 us
  waiting for transfers between devices: 27.3 us -> 52.9 us
  starting transfers between devices: 12.3 us -> 24.4 us
  Pallas kernels: 16.2 us -> 6.05 us
  local copies, waits for them, and re-layouts: 4.57 us -> 10.4 us
  other arithmetic: 4.45 us -> 2.5 us
    all_to_all x0 -> x2, waiting for transfers between devices: none -> 36.3 us  [the longest x1 28.9 us: per_device(): lax.all_to_all(jnp.broadcast_to(mine, (rings,) + mine.shape[1:]), 'row',...]
    all_to_all x1 -> x0, blocking collectives: 32.3 us -> none  [per_device(): lax.all_to_all(jnp.broadcast_to(mine, (rings,) + mine.shape[1:]), 'row',...]
    all_gather x1, waiting for transfers between devices: 18.5 us -> 1.46 us  [per_device(): a_all = lax.all_gather(a_blocks, ('z', 'core'), axis=0, tiled=False)]
    all_to_all x0 -> x2, starting transfers between devices: none -> 12.1 us  [the longest x1 6.79 us: per_device(): lax.all_to_all(jnp.broadcast_to(mine, (rings,) + mine.shape[1:]), 'row',...]
    pallas_call x1, Pallas kernels: 13.9 us -> 3.76 us  [partial_product(): pl.pallas_call(product_kernel, grid=(rows // part,), in_specs=[pl.BlockSp...]
    all_gather x1, waiting for transfers between devices: 6.56 us -> 13.5 us  [per_device(): lax.all_gather(jnp.where(core == x // 2, own, got), ('z', 'core'), axis=0...]
    unnamed x2 -> x4, local copies, waits for them, and re-layouts: 1.59 us -> 4.97 us
    all_to_all x1, blocking collectives: 15.7 us -> 18.1 us  [per_device(): coarse = lax.all_to_all(coarse, 'row', 0, 0, tiled=True)]
  transfers between devices with their start and end apart: 4 -> 6, of which waited for: 4 -> 5; matrix products, arithmetic and copies ran while one was open for 3% -> 5% of each run, Pallas kernels for 10% -> 3%
where the time goes in v2:
time: 147 us; the launch traced here: 146 us
  waiting for transfers between devices  52.9 us (36%)
  blocking collectives  36.5 us (25%)
  starting transfers between devices  24.4 us (17%)
  between operations  13.5 us (9%)
  local copies, waits for them, and re-layouts  10.4 us (7%)
  Pallas kernels  6.05 us (4%)
  other arithmetic  2.5 us (2%)
    all_to_all x1, waiting for transfers between devices, per_device(): lax.all_to_all(jnp.broadcast_to(mine, (rings,) + mine.shape[1:]), 'row',...  28.9 us
    all_to_all x1, blocking collectives, per_device(): swapped = lax.all_to_all(terms, 'rep', 0, 0, tiled=True)  18.4 us
    all_to_all x1, blocking collectives, per_device(): coarse = lax.all_to_all(coarse, 'row', 0, 0, tiled=True)  18.1 us
    all_gather x1, waiting for transfers between devices, per_device(): lax.all_gather(jnp.where(core == x // 2, own, got), ('z', 'core'), axis=0...  13.5 us
    ppermute x1, starting transfers between devices, per_device(): got = lax.ppermute(other, 'core', [(0, 1), (1, 0)])  8.79 us
    all_to_all x1, waiting for transfers between devices, per_device(): lax.all_to_all(jnp.broadcast_to(a_pattern[None], (columns,) + a_pattern.s...  7.35 us
    all_to_all x1, starting transfers between devices, per_device(): lax.all_to_all(jnp.broadcast_to(mine, (rings,) + mine.shape[1:]), 'row',...  6.79 us
    all_to_all x1, starting transfers between devices, per_device(): lax.all_to_all(jnp.broadcast_to(a_pattern[None], (columns,) + a_pattern.s...  5.32 us
  transfers between devices with their start and end apart: 6, of which 5 were waited for; matrix products, arithmetic and copies ran while one was open for 5% of the time, Pallas kernels for 3%

profile of v2, /device:TPU:1, one launch (start us, length us, event | category | flops | bytes accessed | tf_op | source)
XLA Modules:
  0.0 146.3 jit_solution(2366277353671216483)
XLA Ops:
  6.5 0.7 all-gather.7.cloned.1.call-update
  7.3 0.7 broadcast_compare_fusion
  8.1 1.1 broadcast_select_fusion
  9.5 2.0 %copy.13 = bf16[16,64,2,64]{3,2,1,0:T(2,128)(2,1)S(1)} copy(bf16[16,64,2,64]{1,2,3,0:T(2,128)(2,1)S(1)} %bitcast.20) | data formatting | bytes 524288 | tf_op jit(solution)/shard_map/transpose | solution.py:128
  11.8 8.8 %collective-permute-start = (bf16[8,64,128]{2,1,0:T(8,128)(2,1)S(1)}, bf16[8,64,128]{2,1,0:T(8,128)(2,1)S(1)}, u32[]{:S(2)}, u32[]{:S(2)}) collective-permute-start(bf16[8,64,128]{2,1,0:T(8,128)(2,1)S(1)} %dynamic-slice_bitcast_fusion.1), channel_id=1, source_target_pairs={{0,4},{4,0},{1,5},{5,1},{2,6},{6,2},{3,7},{7,3},{8,12},{12,8},{9,1... | collective-permute-start | bytes 393224 | tf_op jit(solution)/shard_map/ppermute | solution.py:153
  20.6 0.9 collective-permute-done
  21.6 0.7 bitcast_select_fusion
  22.3 1.3 broadcast_in_dim.27
  23.6 5.3 %all-to-all-start = ((s32[16,16,2]{1,2,0:T(2,128)}), s32[16,16,2]{1,2,0:T(2,128)S(1)}, u32[]{:S(2)}, u32[]{:S(2)}) async-start(s32[16,16,2]{1,2,0:T(2,128)} %broadcast_in_dim.27), calls=%async_computation | async-start | bytes 32768 | tf_op jit(solution)/shard_map/all_to_all | solution.py:137
  28.9 7.3 %all-to-all-done = s32[16,16,2]{1,2,0:T(2,128)S(1)} async-done(((s32[16,16,2]{1,2,0:T(2,128)}), s32[16,16,2]{1,2,0:T(2,128)S(1)}, u32[]{:S(2)}, u32[]{:S(2)}) %all-to-all-start) | async-done | bytes 2080 | tf_op jit(solution)/shard_map/all_to_all | solution.py:137
  36.2 1.2 broadcast_in_dim.29
  37.5 6.8 %all-to-all-start.1 = ((bf16[8,2,2,2,64,128]{5,4,3,2,1,0:T(8,128)(2,1)}), bf16[8,2,2,2,64,128]{5,4,3,2,1,0:T(8,128)(2,1)S(1)}, u32[]{:S(2)}, u32[]{:S(2)}) async-start(bf16[8,2,2,2,64,128]{5,4,3,2,1,0:T(8,128)(2,1)} %broadcast_in_dim.29), calls=%async_computation.1 | async-start | bytes 2097152 | tf_op jit(solution)/shard_map/all_to_all | solution.py:145
  44.6 28.9 %all-to-all-done.1 = bf16[8,2,2,2,64,128]{5,4,3,2,1,0:T(8,128)(2,1)S(1)} async-done(((bf16[8,2,2,2,64,128]{5,4,3,2,1,0:T(8,128)(2,1)}), bf16[8,2,2,2,64,128]{5,4,3,2,1,0:T(8,128)(2,1)S(1)}, u32[]{:S(2)}, u32[]{:S(2)}) %all-to-all-start.1) | async-done | bytes 1048608 | tf_op jit(solution)/shard_map/all_to_all | solution.py:145
  73.5 1.5 %all-gather.7.cloned.1.call-done = bf16[256,2,64,128]{3,2,1,0:T(8,128)(2,1)} async-done(((bf16[16,2,64,128]{3,2,1,0:T(8,128)(2,1)}), bf16[256,2,64,128]{3,2,1,0:T(8,128)(2,1)}) %all-gather.7.cloned.1.call-update) | async-done | bytes 8388624 | tf_op jit(solution)/shard_map/all_gather | solution.py:135
  75.0 3.4 %copy-done = bf16[256,2,64,128]{3,2,1,0:T(8,128)(2,1)S(1)} copy-done((bf16[256,2,64,128]{3,2,1,0:T(8,128)(2,1)S(1)}, bf16[256,2,64,128]{3,2,1,0:T(8,128)(2,1)}, u32[]{:S(2)}) %copy-start) | copy-done | bytes 8388632
  78.4 3.8 %product_terms.1 = f32[16,2,64,128]{3,2,1,0:T(8,128)S(1)} custom-call(s32[512]{0:T(512)S(1)} %reshape.29.pattern_ref, bf16[16,16,2,64,128]{4,3,2,1,0:T(8,128)(2,1)S(1)} %bitcast.15, bf16[16,2,2,64,128]{4,3,2,1,0:T(8,128)(2,1)S(1)} %bitcast.17), custom_call_target="tpu_custom_call" | custom-call | tf_op jit(solution)/shard_map/product_terms/pallas_call | solution.py:60
  82.1 18.4 %all_to_all.25 = f32[16,2,64,128]{3,2,1,0:T(8,128)S(1)} all-to-all(f32[16,2,64,128]{3,2,1,0:T(8,128)S(1)} %product_terms.1), channel_id=1, replica_groups=mesh['row'=8,'z'=8,'core'=2,'rep'=4] {'rep'}, dimensions={0} | all-to-all | bytes 2097152 | tf_op jit(solution)/shard_map/all_to_all | solution.py:159
  100.5 0.8 shard_map.46
  101.4 3.5 %all-to-all-start.3 = ((bf16[4,4,2,64,128]{4,3,2,1,0:T(8,128)(2,1)}), bf16[4,4,2,64,128]{4,3,2,1,0:T(8,128)(2,1)S(1)}, u32[]{:S(2)}, u32[]{:S(2)}) async-start(bf16[4,4,2,64,128]{4,3,2,1,0:T(8,128)(2,1)} %shard_map.46), calls=%async_computation.3 | async-start | bytes 1048576 | tf_op jit(solution)/shard_map/all_to_all | solution.py:166
  104.9 13.5 %all-gather.5.cloned.1.call-done = bf16[128,64,128]{2,1,0:T(8,128)(2,1)} async-done(((bf16[8,64,128]{2,1,0:T(8,128)(2,1)}), bf16[128,64,128]{2,1,0:T(8,128)(2,1)}) %all-gather.5.cloned.1.call-update) | async-done | bytes 2097168 | tf_op jit(solution)/shard_map/all_gather | solution.py:154
  118.4 1.6 %copy-done.1 = bf16[128,64,128]{2,1,0:T(8,128)(2,1)S(1)} copy-done((bf16[128,64,128]{2,1,0:T(8,128)(2,1)S(1)}, bf16[128,64,128]{2,1,0:T(8,128)(2,1)}, u32[]{:S(2)}) %copy-start.1) | copy-done | bytes 2097176
  119.9 0.8 shard_map.47
  120.7 18.1 %all_to_all.26.in_ref = bf16[8,2,64,128]{3,2,1,0:T(8,128)(2,1)S(1)} all-to-all(bf16[8,2,64,128]{3,2,1,0:T(8,128)(2,1)S(1)} %shard_map.47), channel_id=1, replica_groups=mesh['row'=8,'z'=8,'core'=2,'rep'=4] {'row'}, dimensions={0} | all-to-all | bytes 524288 | tf_op jit(solution)/shard_map/all_to_all | solution.py:173
  138.8 0.7 shard_map.48
  (14 shorter events, 1.0 us)
Async XLA Ops:
  6.5 68.4 %all-gather.7.cloned.1.call-start = ((), (), s32[]{:S(2)}) async-start(), calls=%async_computation.6 | async-start | bytes 8912896 | tf_op jit(solution)/shard_map/all_gather | solution.py:135
  7.3 111.1 %all-gather.5.cloned.1.call-start = ((), (), s32[]{:S(2)}) async-start(), calls=%async_computation.5 | async-start | bytes 2228224 | tf_op jit(solution)/shard_map/all_gather | solution.py:154
  11.8 9.8 %collective-permute-start = (bf16[8,64,128]{2,1,0:T(8,128)(2,1)S(1)}, bf16[8,64,128]{2,1,0:T(8,128)(2,1)S(1)}, u32[]{:S(2)}, u32[]{:S(2)}) collective-permute-start(bf16[8,64,128]{2,1,0:T(8,128)(2,1)S(1)} %dynamic-slice_bitcast_fusion.1), channel_id=1, source_target_pairs={{0,4},{4,0},{1,5},{5,1},{2,6},{6,2},{3,7},{7,3},{8,12},{12,8},{9,1... | collective-permute-start | bytes 393224 | tf_op jit(solution)/shard_map/ppermute | solution.py:153
  23.6 12.7 %all-to-all-start = ((s32[16,16,2]{1,2,0:T(2,128)}), s32[16,16,2]{1,2,0:T(2,128)S(1)}, u32[]{:S(2)}, u32[]{:S(2)}) async-start(s32[16,16,2]{1,2,0:T(2,128)} %broadcast_in_dim.27), calls=%async_computation | async-start | bytes 32768 | tf_op jit(solution)/shard_map/all_to_all | solution.py:137
  37.5 36.0 %all-to-all-start.1 = ((bf16[8,2,2,2,64,128]{5,4,3,2,1,0:T(8,128)(2,1)}), bf16[8,2,2,2,64,128]{5,4,3,2,1,0:T(8,128)(2,1)S(1)}, u32[]{:S(2)}, u32[]{:S(2)}) async-start(bf16[8,2,2,2,64,128]{5,4,3,2,1,0:T(8,128)(2,1)} %broadcast_in_dim.29), calls=%async_computation.1 | async-start | bytes 2097152 | tf_op jit(solution)/shard_map/all_to_all | solution.py:145
  75.0 3.4 %copy-start = (bf16[256,2,64,128]{3,2,1,0:T(8,128)(2,1)S(1)}, bf16[256,2,64,128]{3,2,1,0:T(8,128)(2,1)}, u32[]{:S(2)}) copy-start(bf16[256,2,64,128]{3,2,1,0:T(8,128)(2,1)} %all-gather.7.cloned.1.call-done) | copy-start | bytes 25165828
  101.4 17.0 %all-to-all-start.3 = ((bf16[4,4,2,64,128]{4,3,2,1,0:T(8,128)(2,1)}), bf16[4,4,2,64,128]{4,3,2,1,0:T(8,128)(2,1)S(1)}, u32[]{:S(2)}, u32[]{:S(2)}) async-start(bf16[4,4,2,64,128]{4,3,2,1,0:T(8,128)(2,1)} %shard_map.46), calls=%async_computation.3 | async-start | bytes 1048576 | tf_op jit(solution)/shard_map/all_to_all | solution.py:166
  118.4 1.6 %copy-start.1 = (bf16[128,64,128]{2,1,0:T(8,128)(2,1)S(1)}, bf16[128,64,128]{2,1,0:T(8,128)(2,1)}, u32[]{:S(2)}) copy-start(bf16[128,64,128]{2,1,0:T(8,128)(2,1)} %all-gather.5.cloned.1.call-done) | copy-start | bytes 6291460
Sparse Core Ops, SparseCore 0:
  9.5 65.4 all-gather.6
  77.1 41.2 all-gather.4

commit v3 on v2

--- a/solution.py
+++ b/solution.py
@@ -132,10 +132,10 @@
     x = lax.axis_index("rep")
     core = lax.axis_index("core")
     layers, rings = lax.axis_size("rep"), lax.axis_size("row")
-    a_all = lax.all_gather(a_blocks, ("z", "core"), axis=0, tiled=False)
-    columns = 2 * lax.axis_size("z")
+    a_all = lax.all_gather(a_blocks, ("pair", "odd", "core"), axis=0, tiled=False)
+    columns = 2 * lax.axis_size("pair") * lax.axis_size("odd")
     kept = lax.all_to_all(
-        jnp.broadcast_to(a_pattern[None], (columns,) + a_pattern.shape), ("z", "core"), 0, 0, tiled=True
+        jnp.broadcast_to(a_pattern[None], (columns,) + a_pattern.shape), ("pair", "odd", "core"), 0, 0, tiled=True
     )
     p_live = jnp.where(p_pattern[:, :, None, None] > 0, p_blocks, jnp.zeros_like(p_blocks))
 
@@ -147,12 +147,12 @@
     )
 
     column = lax.dynamic_index_in_dim(p_live, x % 2, axis=1, keepdims=False)
-    column = transposed(column).reshape(2, 8, BLOCK, 2 * BLOCK)
-    own = lax.dynamic_index_in_dim(column, core, axis=0, keepdims=False)
-    other = lax.dynamic_index_in_dim(column, 1 - core, axis=0, keepdims=False)
-    got = lax.ppermute(other, "core", [(0, 1), (1, 0)])
+    column = transposed(column)
+    other = lax.ppermute(column, "core", [(0, 1), (1, 0)])
+    column = jnp.where(core == x // 2, column, other)
+    beside = lax.ppermute(column, ("odd", "core"), [(0, 2), (3, 1)])
     left = lax.all_gather(
-        jnp.where(core == x // 2, own, got), ("z", "core"), axis=0, tiled=False
+        jnp.where(lax.axis_index("odd") == core, column, beside), ("pair", "core"), axis=0, tiled=False
     ).reshape(8, 2, 8, BLOCK, 2 * BLOCK)
 
     terms = partial_product(kept.reshape(-1), a_all, met.reshape(2 * rings, 2, 2, BLOCK, 2 * BLOCK))
@@ -176,16 +176,17 @@
 
 def solution(mesh):
     rows, cols, reps = (mesh.shape[name] for name in ("row", "col", "rep"))
-    fine = Mesh(mesh.devices.reshape(rows, cols // 2, 2, reps), ("row", "z", "core", "rep"))
+    shape = (rows, cols // 4, 2, 2, reps)
+    fine = Mesh(mesh.devices.reshape(shape), ("row", "pair", "odd", "core", "rep"))
     return jax.shard_map(
         per_device,
         mesh=fine,
         in_specs=(
-            P("row", ("z", "core", "rep"), None, None),
-            P("row", ("z", "core", "rep")),
-            P("row", ("z", "core"), None, None),
-            P("row", ("z", "core")),
+            P("row", ("pair", "odd", "core", "rep"), None, None),
+            P("row", ("pair", "odd", "core", "rep")),
+            P("row", ("pair", "odd", "core"), None, None),
+            P("row", ("pair", "odd", "core")),
         ),
-        out_specs=P(("row", "rep"), ("z", "core"), None, None),
+        out_specs=P(("row", "rep"), ("pair", "odd", "core"), None, None),
         check_vma=False,
     )

time: 147 us -> 143 us (0.973); the launches traced: 146 us -> 140 us
  blocking collectives: 36.5 us -> 29.8 us
  starting transfers between devices: 24.4 us -> 26.9 us
  waiting for transfers between devices: 52.9 us -> 51.2 us
    all_gather x2, waiting for transfers between devices: 14.9 us -> 3.85 us  [the longest x1 3.84 us: per_device(): lax.all_gather(jnp.where(lax.axis_index('odd') == core, column, beside),...]
    all_to_all x1, blocking collectives: 18.1 us -> 11.8 us  [per_device(): coarse = lax.all_to_all(coarse, 'row', 0, 0, tiled=True)]
    ppermute x1 -> x2, waiting for transfers between devices: 0.95 us -> 6.93 us  [the longest x1 5.81 us: per_device(): beside = lax.ppermute(column, ('odd', 'core'), [(0, 2), (3, 1)])]
    all_to_all x1, waiting for transfers between devices: 0.01 us -> 3.39 us  [per_device(): product = lax.all_to_all(product, 'rep', 0, 0, tiled=True)]
    ppermute x1 -> x2, starting transfers between devices: 8.79 us -> 10.1 us  [the longest x1 8.79 us: per_device(): other = lax.ppermute(column, 'core', [(0, 1), (1, 0)])]
  transfers between devices with their start and end apart: 6 -> 7, of which waited for: 5 -> 6; matrix products, arithmetic and copies ran while one was open for 5% -> 6% of each run, Pallas kernels for 3% -> 3%
where the time goes in v3:
time: 143 us; the launch traced here: 140 us
  waiting for transfers between devices  51.2 us (36%)
  blocking collectives  29.8 us (21%)
  starting transfers between devices  26.9 us (19%)
  between operations  13.5 us (9%)
  local copies, waits for them, and re-layouts  10.4 us (7%)
  Pallas kernels  6.05 us (4%)
  other arithmetic  2.58 us (2%)
    all_to_all x1, waiting for transfers between devices, per_device(): lax.all_to_all(jnp.broadcast_to(mine, (rings,) + mine.shape[1:]), 'row',...  28.9 us
    all_to_all x1, blocking collectives, per_device(): swapped = lax.all_to_all(terms, 'rep', 0, 0, tiled=True)  17.9 us
    all_to_all x1, blocking collectives, per_device(): coarse = lax.all_to_all(coarse, 'row', 0, 0, tiled=True)  11.8 us
    ppermute x1, starting transfers between devices, per_device(): other = lax.ppermute(column, 'core', [(0, 1), (1, 0)])  8.79 us
    all_to_all x1, waiting for transfers between devices, per_device(): lax.all_to_all(jnp.broadcast_to(a_pattern[None], (columns,) + a_pattern.s...  7.37 us
    all_to_all x1, starting transfers between devices, per_device(): lax.all_to_all(jnp.broadcast_to(mine, (rings,) + mine.shape[1:]), 'row',...  6.83 us
    all_to_all x1, starting transfers between devices, per_device(): lax.all_to_all(jnp.broadcast_to(a_pattern[None], (columns,) + a_pattern.s...  6.48 us
    ppermute x1, waiting for transfers between devices, per_device(): beside = lax.ppermute(column, ('odd', 'core'), [(0, 2), (3, 1)])  5.81 us
  transfers between devices with their start and end apart: 7, of which 6 were waited for; matrix products, arithmetic and copies ran while one was open for 6% of the time, Pallas kernels for 3%

profile of v3, /device:TPU:1, one launch (start us, length us, event | category | flops | bytes accessed | tf_op | source)
XLA Modules:
  0.0 140.4 jit_solution(678340375374553371)
XLA Ops:
  6.5 0.7 all-gather.7.cloned.1.call-update
  8.1 1.1 broadcast_select_fusion
  9.5 2.0 %copy.13 = bf16[16,64,2,64]{3,2,1,0:T(2,128)(2,1)S(1)} copy(bf16[16,64,2,64]{1,2,3,0:T(2,128)(2,1)S(1)} %bitcast.16) | data formatting | bytes 524288 | tf_op jit(solution)/shard_map/transpose | solution.py:128
  11.8 8.8 %collective-permute-start = (bf16[16,64,128]{2,1,0:T(8,128)(2,1)S(1)}, bf16[16,64,128]{2,1,0:T(8,128)(2,1)S(1)}, u32[]{:S(2)}, u32[]{:S(2)}) collective-permute-start(bf16[16,64,128]{2,1,0:T(8,128)(2,1)S(1)} %reshape.31), channel_id=1, source_target_pairs={{0,4},{4,0},{1,5},{5,1},{2,6},{6,2},{3,7},{7,3},{8,12},{12,8},{9,1... | collective-permute-start | bytes 786440 | tf_op jit(solution)/shard_map/ppermute | solution.py:151
  20.6 1.1 collective-permute-done
  21.8 1.3 collective-permute-start.1
  23.1 5.8 %collective-permute-done.1 = bf16[16,64,128]{2,1,0:T(8,128)(2,1)S(1)} collective-permute-done((bf16[16,64,128]{2,1,0:T(8,128)(2,1)S(1)}, bf16[16,64,128]{2,1,0:T(8,128)(2,1)S(1)}, u32[]{:S(2)}, u32[]{:S(2)}) %collective-permute-start.1) | collective-permute-done | bytes 262176 | tf_op jit(solution)/shard_map/ppermute | solution.py:153
  28.9 0.7 broadcast_select_fusion.2
  29.6 1.3 broadcast_in_dim.27
  30.9 6.5 %all-to-all-start = ((s32[16,16,2]{1,2,0:T(2,128)}), s32[16,16,2]{1,2,0:T(2,128)S(1)}, u32[]{:S(2)}, u32[]{:S(2)}) async-start(s32[16,16,2]{1,2,0:T(2,128)} %broadcast_in_dim.27), calls=%async_computation | async-start | bytes 32768 | tf_op jit(solution)/shard_map/all_to_all | solution.py:137
  37.4 7.4 %all-to-all-done = s32[16,16,2]{1,2,0:T(2,128)S(1)} async-done(((s32[16,16,2]{1,2,0:T(2,128)}), s32[16,16,2]{1,2,0:T(2,128)S(1)}, u32[]{:S(2)}, u32[]{:S(2)}) %all-to-all-start) | async-done | bytes 2080 | tf_op jit(solution)/shard_map/all_to_all | solution.py:137
  44.8 1.2 broadcast_in_dim.29
  46.0 6.8 %all-to-all-start.1 = ((bf16[8,2,2,2,64,128]{5,4,3,2,1,0:T(8,128)(2,1)}), bf16[8,2,2,2,64,128]{5,4,3,2,1,0:T(8,128)(2,1)S(1)}, u32[]{:S(2)}, u32[]{:S(2)}) async-start(bf16[8,2,2,2,64,128]{5,4,3,2,1,0:T(8,128)(2,1)} %broadcast_in_dim.29), calls=%async_computation.1 | async-start | bytes 2097152 | tf_op jit(solution)/shard_map/all_to_all | solution.py:145
  53.1 28.9 %all-to-all-done.1 = bf16[8,2,2,2,64,128]{5,4,3,2,1,0:T(8,128)(2,1)S(1)} async-done(((bf16[8,2,2,2,64,128]{5,4,3,2,1,0:T(8,128)(2,1)}), bf16[8,2,2,2,64,128]{5,4,3,2,1,0:T(8,128)(2,1)S(1)}, u32[]{:S(2)}, u32[]{:S(2)}) %all-to-all-start.1) | async-done | bytes 1048608 | tf_op jit(solution)/shard_map/all_to_all | solution.py:145
  82.1 3.4 %copy-done = bf16[256,2,64,128]{3,2,1,0:T(8,128)(2,1)S(1)} copy-done((bf16[256,2,64,128]{3,2,1,0:T(8,128)(2,1)S(1)}, bf16[256,2,64,128]{3,2,1,0:T(8,128)(2,1)}, u32[]{:S(2)}) %copy-start) | copy-done | bytes 8388632
  85.5 3.8 %product_terms.1 = f32[16,2,64,128]{3,2,1,0:T(8,128)S(1)} custom-call(s32[512]{0:T(512)S(1)} %reshape.33.pattern_ref, bf16[16,16,2,64,128]{4,3,2,1,0:T(8,128)(2,1)S(1)} %bitcast.11, bf16[16,2,2,64,128]{4,3,2,1,0:T(8,128)(2,1)S(1)} %bitcast.13), custom_call_target="tpu_custom_call" | custom-call | tf_op jit(solution)/shard_map/product_terms/pallas_call | solution.py:60
  89.2 17.9 %all_to_all.25 = f32[16,2,64,128]{3,2,1,0:T(8,128)S(1)} all-to-all(f32[16,2,64,128]{3,2,1,0:T(8,128)S(1)} %product_terms.1), channel_id=1, replica_groups=mesh['row'=8,'pair'=4,'odd'=2,'core'=2,'rep'=4] {'rep'}, dimensions={0} | all-to-all | bytes 2097152 | tf_op jit(solution)/shard_map/all_to_all | solution.py:159
  107.1 0.8 shard_map.46
  108.0 3.5 %all-to-all-start.3 = ((bf16[4,4,2,64,128]{4,3,2,1,0:T(8,128)(2,1)}), bf16[4,4,2,64,128]{4,3,2,1,0:T(8,128)(2,1)S(1)}, u32[]{:S(2)}, u32[]{:S(2)}) async-start(bf16[4,4,2,64,128]{4,3,2,1,0:T(8,128)(2,1)} %shard_map.46), calls=%async_computation.3 | async-start | bytes 1048576 | tf_op jit(solution)/shard_map/all_to_all | solution.py:166
  111.5 3.8 %all-gather.5.cloned.1.call-done = bf16[128,64,128]{2,1,0:T(8,128)(2,1)} async-done(((bf16[16,64,128]{2,1,0:T(8,128)(2,1)}), bf16[128,64,128]{2,1,0:T(8,128)(2,1)}) %all-gather.5.cloned.1.call-update) | async-done | bytes 2097168 | tf_op jit(solution)/shard_map/all_gather | solution.py:154
  115.3 3.4 %all-to-all-done.3 = bf16[4,4,2,64,128]{4,3,2,1,0:T(8,128)(2,1)S(1)} async-done(((bf16[4,4,2,64,128]{4,3,2,1,0:T(8,128)(2,1)}), bf16[4,4,2,64,128]{4,3,2,1,0:T(8,128)(2,1)S(1)}, u32[]{:S(2)}, u32[]{:S(2)}) %all-to-all-start.3) | async-done | bytes 524320 | tf_op jit(solution)/shard_map/all_to_all | solution.py:166
  118.7 1.6 %copy-done.1 = bf16[128,64,128]{2,1,0:T(8,128)(2,1)S(1)} copy-done((bf16[128,64,128]{2,1,0:T(8,128)(2,1)S(1)}, bf16[128,64,128]{2,1,0:T(8,128)(2,1)}, u32[]{:S(2)}) %copy-start.1) | copy-done | bytes 2097176
  120.3 0.8 shard_map.47
  121.1 11.8 %all_to_all.26.in_ref = bf16[8,2,64,128]{3,2,1,0:T(8,128)(2,1)S(1)} all-to-all(bf16[8,2,64,128]{3,2,1,0:T(8,128)(2,1)S(1)} %shard_map.47), channel_id=1, replica_groups=mesh['row'=8,'pair'=4,'odd'=2,'core'=2,'rep'=4] {'row'}, dimensions={0} | all-to-all | bytes 524288 | tf_op jit(solution)/shard_map/all_to_all | solution.py:173
  (16 shorter events, 2.4 us)
Async XLA Ops:
  6.5 75.5 %all-gather.7.cloned.1.call-start = ((), (), s32[]{:S(2)}) async-start(), calls=%async_computation.6 | async-start | bytes 8912896 | tf_op jit(solution)/shard_map/all_gather | solution.py:135
  7.3 108.1 %all-gather.5.cloned.1.call-start = ((), (), s32[]{:S(2)}) async-start(), calls=%async_computation.5 | async-start | bytes 2359296 | tf_op jit(solution)/shard_map/all_gather | solution.py:154
  11.8 9.9 %collective-permute-start = (bf16[16,64,128]{2,1,0:T(8,128)(2,1)S(1)}, bf16[16,64,128]{2,1,0:T(8,128)(2,1)S(1)}, u32[]{:S(2)}, u32[]{:S(2)}) collective-permute-start(bf16[16,64,128]{2,1,0:T(8,128)(2,1)S(1)} %reshape.31), channel_id=1, source_target_pairs={{0,4},{4,0},{1,5},{5,1},{2,6},{6,2},{3,7},{7,3},{8,12},{12,8},{9,1... | collective-permute-start | bytes 786440 | tf_op jit(solution)/shard_map/ppermute | solution.py:151
  21.8 7.1 %collective-permute-start.1 = (bf16[16,64,128]{2,1,0:T(8,128)(2,1)S(1)}, bf16[16,64,128]{2,1,0:T(8,128)(2,1)S(1)}, u32[]{:S(2)}, u32[]{:S(2)}) collective-permute-start(bf16[16,64,128]{2,1,0:T(8,128)(2,1)S(1)} %broadcast_select_fusion.1), channel_id=1, source_target_pairs={{0,8},{12,4},{1,9},{13,5},{2,10},{14,6},{3,11},{15,7},{16,24},{28,... | collective-permute-start | bytes 786440 | tf_op jit(solution)/shard_map/ppermute | solution.py:153
  30.9 13.9 %all-to-all-start = ((s32[16,16,2]{1,2,0:T(2,128)}), s32[16,16,2]{1,2,0:T(2,128)S(1)}, u32[]{:S(2)}, u32[]{:S(2)}) async-start(s32[16,16,2]{1,2,0:T(2,128)} %broadcast_in_dim.27), calls=%async_computation | async-start | bytes 32768 | tf_op jit(solution)/shard_map/all_to_all | solution.py:137
  46.0 36.1 %all-to-all-start.1 = ((bf16[8,2,2,2,64,128]{5,4,3,2,1,0:T(8,128)(2,1)}), bf16[8,2,2,2,64,128]{5,4,3,2,1,0:T(8,128)(2,1)S(1)}, u32[]{:S(2)}, u32[]{:S(2)}) async-start(bf16[8,2,2,2,64,128]{5,4,3,2,1,0:T(8,128)(2,1)} %broadcast_in_dim.29), calls=%async_computation.1 | async-start | bytes 2097152 | tf_op jit(solution)/shard_map/all_to_all | solution.py:145
  82.1 3.4 %copy-start = (bf16[256,2,64,128]{3,2,1,0:T(8,128)(2,1)S(1)}, bf16[256,2,64,128]{3,2,1,0:T(8,128)(2,1)}, u32[]{:S(2)}) copy-start(bf16[256,2,64,128]{3,2,1,0:T(8,128)(2,1)} %all-gather.7.cloned.1.call-done) | copy-start | bytes 25165828
  108.0 10.7 %all-to-all-start.3 = ((bf16[4,4,2,64,128]{4,3,2,1,0:T(8,128)(2,1)}), bf16[4,4,2,64,128]{4,3,2,1,0:T(8,128)(2,1)S(1)}, u32[]{:S(2)}, u32[]{:S(2)}) async-start(bf16[4,4,2,64,128]{4,3,2,1,0:T(8,128)(2,1)} %shard_map.46), calls=%async_computation.3 | async-start | bytes 1048576 | tf_op jit(solution)/shard_map/all_to_all | solution.py:166
  118.7 1.6 %copy-start.1 = (bf16[128,64,128]{2,1,0:T(8,128)(2,1)S(1)}, bf16[128,64,128]{2,1,0:T(8,128)(2,1)}, u32[]{:S(2)}) copy-start(bf16[128,64,128]{2,1,0:T(8,128)(2,1)} %all-gather.5.cloned.1.call-done) | copy-start | bytes 6291460
Sparse Core Ops, SparseCore 0:
  9.5 65.5 all-gather.6
  77.3 38.0 all-gather.4

commit v4 on v3

--- a/solution.py
+++ b/solution.py
@@ -22,12 +22,10 @@
     return jnp.concatenate([jnp.concatenate([b, lower_half(b)], axis=0) for b in blocks], axis=1)
 
 
-def product_kernel(pattern_ref, a_ref, p_ref, out_ref, right):
+def product_kernel(a_ref, p_ref, out_ref, right):
     groups, part = a_ref.shape[0], a_ref.shape[1]
-    step, steps = pl.program_id(0), pl.num_programs(0)
-    zero = jnp.zeros((BLOCK, 2 * BLOCK), BF16)
 
-    @pl.when(step == 0)
+    @pl.when(pl.program_id(0) == 0)
     def _():
         for g in range(groups):
             right[g] = jnp.concatenate(
@@ -36,32 +34,21 @@
 
     total = jnp.zeros((part * BLOCK, 4 * BLOCK), F32)
     for g in range(groups):
-        at = (g * steps + step) * part * 2
-        sides = [
-            jnp.concatenate(
-                [
-                    jnp.where(pattern_ref[at + 2 * i + e] > 0, a_ref[g, i, e], zero)
-                    for i in range(part)
-                ],
-                axis=0,
-            )
-            for e in range(2)
-        ]
-        total += jnp.dot(
-            jnp.concatenate(sides, axis=1), right[g], preferred_element_type=F32
+        left = jnp.concatenate(
+            [a_ref[g, :, e].reshape(part * BLOCK, 2 * BLOCK) for e in range(2)], axis=1
         )
+        total += jnp.dot(left, right[g], preferred_element_type=F32)
     for b in range(2):
         out_ref[:, b] = total[:, b * 2 * BLOCK : (b + 1) * 2 * BLOCK].reshape(part, BLOCK, 2 * BLOCK)
 
 
-def partial_product(pattern, a_all, p_all, part=8):
+def partial_product(a_all, p_all, part=8):
     groups, rows = a_all.shape[0], a_all.shape[1]
     block = (BLOCK, 2 * BLOCK)
     return pl.pallas_call(
         product_kernel,
         grid=(rows // part,),
         in_specs=[
-            pl.BlockSpec(memory_space=pltpu.SMEM),
             pl.BlockSpec((groups, part, 2) + block, lambda s: (0, s, 0, 0, 0)),
             pl.BlockSpec((groups, 2, 2) + block, lambda s: (0, 0, 0, 0, 0)),
         ],
@@ -70,7 +57,7 @@
         scratch_shapes=[pltpu.VMEM((groups, 4 * BLOCK, 4 * BLOCK), BF16)],
         compiler_params=pltpu.CompilerParams(vmem_limit_bytes=32 * 1024 * 1024),
         name="product_terms",
-    )(pattern, a_all, p_all)
+    )(a_all, p_all)
 
 
 def sum_kernel(copies, in_ref, out_ref):
@@ -132,11 +119,8 @@
     x = lax.axis_index("rep")
     core = lax.axis_index("core")
     layers, rings = lax.axis_size("rep"), lax.axis_size("row")
-    a_all = lax.all_gather(a_blocks, ("pair", "odd", "core"), axis=0, tiled=False)
-    columns = 2 * lax.axis_size("pair") * lax.axis_size("odd")
-    kept = lax.all_to_all(
-        jnp.broadcast_to(a_pattern[None], (columns,) + a_pattern.shape), ("pair", "odd", "core"), 0, 0, tiled=True
-    )
+    a_live = jnp.where(a_pattern[:, :, None, None] > 0, a_blocks, jnp.zeros_like(a_blocks))
+    a_all = lax.all_gather(a_live, ("pair", "odd", "core"), axis=0, tiled=False)
     p_live = jnp.where(p_pattern[:, :, None, None] > 0, p_blocks, jnp.zeros_like(p_blocks))
 
     mine = lax.dynamic_slice_in_dim(
@@ -155,7 +139,7 @@
         jnp.where(lax.axis_index("odd") == core, column, beside), ("pair", "core"), axis=0, tiled=False
     ).reshape(8, 2, 8, BLOCK, 2 * BLOCK)
 
-    terms = partial_product(kept.reshape(-1), a_all, met.reshape(2 * rings, 2, 2, BLOCK, 2 * BLOCK))
+    terms = partial_product(a_all, met.reshape(2 * rings, 2, 2, BLOCK, 2 * BLOCK))
     swapped = lax.all_to_all(terms, "rep", 0, 0, tiled=True)
     share = terms.shape[0] // layers
     product = call(

time: 143 us -> 141 us (0.986)
  blocking collectives: 29.8 us -> 63.4 us
  waiting for transfers between devices: 51.2 us -> 28.9 us
  starting transfers between devices: 26.9 us -> 13.6 us
  other arithmetic: 2.58 us -> 5.23 us
  local copies, waits for them, and re-layouts: 10.4 us -> 7.93 us
    all_to_all x2 -> x0, waiting for transfers between devices: 36.3 us -> none  [the longest x1 28.9 us: per_device(): lax.all_to_all(jnp.broadcast_to(mine, (rings,) + mine.shape[1:]), 'row',...]
    all_to_all x0 -> x1, blocking collectives: none -> 31.3 us  [per_device(): lax.all_to_all(jnp.broadcast_to(mine, (rings,) + mine.shape[1:]), 'row',...]
    all_to_all x2 -> x0, starting transfers between devices: 13.3 us -> none  [the longest x1 6.83 us: per_device(): lax.all_to_all(jnp.broadcast_to(mine, (rings,) + mine.shape[1:]), 'row',...]
    all_gather x1, waiting for transfers between devices: 0.01 us -> 11.5 us  [per_device(): a_all = lax.all_gather(a_live, ('pair', 'odd', 'core'), axis=0, tiled=False)]
    all_gather x1, waiting for transfers between devices: 3.84 us -> 10.5 us  [per_device(): lax.all_gather(jnp.where(lax.axis_index('odd') == core, column, beside),...]
    all_to_all x1, waiting for transfers between devices: 3.39 us -> 0.01 us  [per_device(): product = lax.all_to_all(product, 'rep', 0, 0, tiled=True)]
    select_n x0 -> x1, other arithmetic: none -> 1.95 us  [per_device(): jnp.where(a_pattern[:, :, None, None] > 0, a_blocks, jnp.zeros_like(a_blo...]
    all_to_all x1, blocking collectives: 11.8 us -> 13.6 us  [per_device(): coarse = lax.all_to_all(coarse, 'row', 0, 0, tiled=True)]
  transfers between devices with their start and end apart: 7 -> 5, of which waited for: 6 -> 4; matrix products, arithmetic and copies ran while one was open for 6% -> 4% of each run, Pallas kernels for 3% -> 3%
where the time goes in v4:
time: 141 us; the launch traced here: 138 us
  blocking collectives  63.4 us (45%)
  waiting for transfers between devices  28.9 us (20%)
  starting transfers between devices  13.6 us (10%)
  between operations  13.6 us (10%)
  local copies, waits for them, and re-layouts  7.93 us (6%)
  Pallas kernels  5.73 us (4%)
  other arithmetic  5.23 us (4%)
    all_to_all x1, blocking collectives, per_device(): lax.all_to_all(jnp.broadcast_to(mine, (rings,) + mine.shape[1:]), 'row',...  31.3 us
    all_to_all x1, blocking collectives, per_device(): swapped = lax.all_to_all(terms, 'rep', 0, 0, tiled=True)  18.5 us
    all_to_all x1, blocking collectives, per_device(): coarse = lax.all_to_all(coarse, 'row', 0, 0, tiled=True)  13.6 us
    all_gather x1, waiting for transfers between devices, per_device(): a_all = lax.all_gather(a_live, ('pair', 'odd', 'core'), axis=0, tiled=False)  11.5 us
    all_gather x1, waiting for transfers between devices, per_device(): lax.all_gather(jnp.where(lax.axis_index('odd') == core, column, beside),...  10.5 us
    ppermute x1, starting transfers between devices, per_device(): other = lax.ppermute(column, 'core', [(0, 1), (1, 0)])  8.79 us
    ppermute x1, waiting for transfers between devices, per_device(): beside = lax.ppermute(column, ('odd', 'core'), [(0, 2), (3, 1)])  5.81 us
    unnamed x4, local copies, waits for them, and re-layouts  4.97 us
  transfers between devices with their start and end apart: 5, of which 4 were waited for; matrix products, arithmetic and copies ran while one was open for 4% of the time, Pallas kernels for 3%

profile of v4, /device:TPU:1, one launch (start us, length us, event | category | flops | bytes accessed | tf_op | source)
XLA Modules:
  0.0 138.4 jit_solution(12904940235050230736)
XLA Ops:
  6.5 0.7 broadcast_compare_fusion
  7.3 2.0 %broadcast_select_fusion = bf16[16,2,64,128]{3,2,1,0:T(8,128)(2,1)} fusion(bf16[16,2,64,128]{3,2,1,0:T(8,128)(2,1)} %param.4, pred[16,2]{1,0:T(8,128)(4,1)S(1)} %copy.14), kind=kLoop, calls=%fused_computation | loop fusion | flops 262144 | bytes 1048608 | tf_op jit(solution)/shard_map/jit(_where)/select_n | solution.py:122
  9.4 0.7 broadcast_compare_fusion.1
  10.2 1.1 broadcast_select_fusion.1
  11.3 0.2 reshape.28
  11.6 2.0 %copy.13 = bf16[16,64,2,64]{3,2,1,0:T(2,128)(2,1)S(1)} copy(bf16[16,64,2,64]{1,2,3,0:T(2,128)(2,1)S(1)} %bitcast.16) | data formatting | bytes 524288 | tf_op jit(solution)/shard_map/transpose | solution.py:115
  13.6 0.2 reshape.29
  13.8 8.8 %collective-permute-start = (bf16[16,64,128]{2,1,0:T(8,128)(2,1)S(1)}, bf16[16,64,128]{2,1,0:T(8,128)(2,1)S(1)}, u32[]{:S(2)}, u32[]{:S(2)}) collective-permute-start(bf16[16,64,128]{2,1,0:T(8,128)(2,1)S(1)} %reshape.29), channel_id=1, source_target_pairs={{0,4},{4,0},{1,5},{5,1},{2,6},{6,2},{3,7},{7,3},{8,12},{12,8},{9,1... | collective-permute-start | bytes 786440 | tf_op jit(solution)/shard_map/ppermute | solution.py:135
  22.7 1.1 collective-permute-done
  23.8 1.3 collective-permute-start.1
  25.1 5.8 %collective-permute-done.1 = bf16[16,64,128]{2,1,0:T(8,128)(2,1)S(1)} collective-permute-done((bf16[16,64,128]{2,1,0:T(8,128)(2,1)S(1)}, bf16[16,64,128]{2,1,0:T(8,128)(2,1)S(1)}, u32[]{:S(2)}, u32[]{:S(2)}) %collective-permute-start.1) | collective-permute-done | bytes 262176 | tf_op jit(solution)/shard_map/ppermute | solution.py:137
  30.9 0.7 broadcast_select_fusion.3
  32.0 31.3 %all_to_all.20 = bf16[8,2,2,2,64,128]{5,4,3,2,1,0:T(8,128)(2,1)S(1)} all-to-all(bf16[8,2,2,2,64,128]{5,4,3,2,1,0:T(8,128)(2,1)S(1)} %broadcast_in_dim.25), channel_id=1, replica_groups=mesh['row'=8,'pair'=4,'odd'=2,'core'=2,'rep'=4] {'row'}, dimensions={0} | all-to-all | bytes 2097152 | tf_op jit(solution)/shard_map/all_to_all | solution.py:129
  63.2 11.5 %all-gather.7.cloned.1.call-done = bf16[256,2,64,128]{3,2,1,0:T(8,128)(2,1)} async-done(((bf16[16,2,64,128]{3,2,1,0:T(8,128)(2,1)}), bf16[256,2,64,128]{3,2,1,0:T(8,128)(2,1)}) %all-gather.7.cloned.1.call-update) | async-done | bytes 8388624 | tf_op jit(solution)/shard_map/all_gather | solution.py:123
  74.8 3.4 %copy-done = bf16[256,2,64,128]{3,2,1,0:T(8,128)(2,1)S(1)} copy-done((bf16[256,2,64,128]{3,2,1,0:T(8,128)(2,1)S(1)}, bf16[256,2,64,128]{3,2,1,0:T(8,128)(2,1)}, u32[]{:S(2)}) %copy-start) | copy-done | bytes 8388632
  78.1 3.4 %product_terms.1 = f32[16,2,64,128]{3,2,1,0:T(8,128)S(1)} custom-call(bf16[16,16,2,64,128]{4,3,2,1,0:T(8,128)(2,1)S(1)} %bitcast.11, bf16[16,2,2,64,128]{4,3,2,1,0:T(8,128)(2,1)S(1)} %bitcast.12), custom_call_target="tpu_custom_call" | custom-call | tf_op jit(solution)/shard_map/product_terms/pallas_call | solution.py:48
  81.6 18.5 %all_to_all.21 = f32[16,2,64,128]{3,2,1,0:T(8,128)S(1)} all-to-all(f32[16,2,64,128]{3,2,1,0:T(8,128)S(1)} %product_terms.1), channel_id=1, replica_groups=mesh['row'=8,'pair'=4,'odd'=2,'core'=2,'rep'=4] {'rep'}, dimensions={0} | all-to-all | bytes 2097152 | tf_op jit(solution)/shard_map/all_to_all | solution.py:143
  100.1 0.8 shard_map.46
  101.0 3.5 %all-to-all-start.2 = ((bf16[4,4,2,64,128]{4,3,2,1,0:T(8,128)(2,1)}), bf16[4,4,2,64,128]{4,3,2,1,0:T(8,128)(2,1)S(1)}, u32[]{:S(2)}, u32[]{:S(2)}) async-start(bf16[4,4,2,64,128]{4,3,2,1,0:T(8,128)(2,1)} %shard_map.46), calls=%async_computation.2 | async-start | bytes 1048576 | tf_op jit(solution)/shard_map/all_to_all | solution.py:150
  104.5 10.5 %all-gather.5.cloned.1.call-done = bf16[128,64,128]{2,1,0:T(8,128)(2,1)} async-done(((bf16[16,64,128]{2,1,0:T(8,128)(2,1)}), bf16[128,64,128]{2,1,0:T(8,128)(2,1)}) %all-gather.5.cloned.1.call-update) | async-done | bytes 2097168 | tf_op jit(solution)/shard_map/all_gather | solution.py:138
  114.9 1.6 %copy-done.1 = bf16[128,64,128]{2,1,0:T(8,128)(2,1)S(1)} copy-done((bf16[128,64,128]{2,1,0:T(8,128)(2,1)S(1)}, bf16[128,64,128]{2,1,0:T(8,128)(2,1)}, u32[]{:S(2)}) %copy-start.1) | copy-done | bytes 2097176
  116.5 0.8 shard_map.47
  117.3 13.6 %all_to_all.22.in_ref = bf16[8,2,64,128]{3,2,1,0:T(8,128)(2,1)S(1)} all-to-all(bf16[8,2,64,128]{3,2,1,0:T(8,128)(2,1)S(1)} %shard_map.47), channel_id=1, replica_groups=mesh['row'=8,'pair'=4,'odd'=2,'core'=2,'rep'=4] {'row'}, dimensions={0} | all-to-all | bytes 524288 | tf_op jit(solution)/shard_map/all_to_all | solution.py:157
  130.9 0.7 shard_map.48
  (13 shorter events, 0.6 us)
Async XLA Ops:
  6.5 68.2 %all-gather.7.cloned.1.call-start = ((), (), s32[]{:S(2)}) async-start(), calls=%async_computation.5 | async-start | bytes 8912896 | tf_op jit(solution)/shard_map/all_gather | solution.py:123
  9.3 105.6 %all-gather.5.cloned.1.call-start = ((), (), s32[]{:S(2)}) async-start(), calls=%async_computation.4 | async-start | bytes 2359296 | tf_op jit(solution)/shard_map/all_gather | solution.py:138
  13.8 9.9 %collective-permute-start = (bf16[16,64,128]{2,1,0:T(8,128)(2,1)S(1)}, bf16[16,64,128]{2,1,0:T(8,128)(2,1)S(1)}, u32[]{:S(2)}, u32[]{:S(2)}) collective-permute-start(bf16[16,64,128]{2,1,0:T(8,128)(2,1)S(1)} %reshape.29), channel_id=1, source_target_pairs={{0,4},{4,0},{1,5},{5,1},{2,6},{6,2},{3,7},{7,3},{8,12},{12,8},{9,1... | collective-permute-start | bytes 786440 | tf_op jit(solution)/shard_map/ppermute | solution.py:135
  23.8 7.1 %collective-permute-start.1 = (bf16[16,64,128]{2,1,0:T(8,128)(2,1)S(1)}, bf16[16,64,128]{2,1,0:T(8,128)(2,1)S(1)}, u32[]{:S(2)}, u32[]{:S(2)}) collective-permute-start(bf16[16,64,128]{2,1,0:T(8,128)(2,1)S(1)} %broadcast_select_fusion.2), channel_id=1, source_target_pairs={{0,8},{12,4},{1,9},{13,5},{2,10},{14,6},{3,11},{15,7},{16,24},{28,... | collective-permute-start | bytes 786440 | tf_op jit(solution)/shard_map/ppermute | solution.py:137
  74.8 3.4 %copy-start = (bf16[256,2,64,128]{3,2,1,0:T(8,128)(2,1)S(1)}, bf16[256,2,64,128]{3,2,1,0:T(8,128)(2,1)}, u32[]{:S(2)}) copy-start(bf16[256,2,64,128]{3,2,1,0:T(8,128)(2,1)} %all-gather.7.cloned.1.call-done) | copy-start | bytes 25165828
  101.0 13.9 %all-to-all-start.2 = ((bf16[4,4,2,64,128]{4,3,2,1,0:T(8,128)(2,1)}), bf16[4,4,2,64,128]{4,3,2,1,0:T(8,128)(2,1)S(1)}, u32[]{:S(2)}, u32[]{:S(2)}) async-start(bf16[4,4,2,64,128]{4,3,2,1,0:T(8,128)(2,1)} %shard_map.46), calls=%async_computation.2 | async-start | bytes 1048576 | tf_op jit(solution)/shard_map/all_to_all | solution.py:150
  114.9 1.6 %copy-start.1 = (bf16[128,64,128]{2,1,0:T(8,128)(2,1)S(1)}, bf16[128,64,128]{2,1,0:T(8,128)(2,1)}, u32[]{:S(2)}) copy-start(bf16[128,64,128]{2,1,0:T(8,128)(2,1)} %all-gather.5.cloned.1.call-done) | copy-start | bytes 6291460
Sparse Core Ops, SparseCore 0:
  9.5 65.2 all-gather.6
  76.9 37.9 all-gather.4

commit v5 on v4

--- a/solution.py
+++ b/solution.py
@@ -72,16 +72,16 @@
 def coarse_kernel(left_ref, prod_ref, out_ref):
     groups = left_ref.shape[0]
     total = jnp.zeros((groups * BLOCK, 4 * BLOCK), F32)
-    for i in range(0, prod_ref.shape[0], 2):
+    for i in range(0, prod_ref.shape[0], 4):
         left = jnp.concatenate(
             [
                 left_ref[:, (i + e) // 8, (i + e) % 8].reshape(groups * BLOCK, 2 * BLOCK)
-                for e in range(2)
+                for e in range(4)
             ],
             axis=1,
         )
         right = jnp.concatenate(
-            [real_pair([prod_ref[i + e, 0], prod_ref[i + e, 1]]) for e in range(2)], axis=0
+            [real_pair([prod_ref[i + e, 0], prod_ref[i + e, 1]]) for e in range(4)], axis=0
         )
         total = total + jnp.dot(left, right, preferred_element_type=F32)
     for b in range(2):

time: 141 us -> 141 us (level)
  no operation moved by 1% of the time
where the time goes in v5:
time: 141 us; the launch traced here: 138 us
  blocking collectives  63.4 us (45%)
  waiting for transfers between devices  28.9 us (20%)
  starting transfers between devices  13.6 us (10%)
  between operations  13.6 us (10%)
  local copies, waits for them, and re-layouts  7.93 us (6%)
  Pallas kernels  5.73 us (4%)
  other arithmetic  5.23 us (4%)
    all_to_all x1, blocking collectives, per_device(): lax.all_to_all(jnp.broadcast_to(mine, (rings,) + mine.shape[1:]), 'row',...  31.3 us
    all_to_all x1, blocking collectives, per_device(): swapped = lax.all_to_all(terms, 'rep', 0, 0, tiled=True)  18.5 us
    all_to_all x1, blocking collectives, per_device(): coarse = lax.all_to_all(coarse, 'row', 0, 0, tiled=True)  13.6 us
    all_gather x1, waiting for transfers between devices, per_device(): a_all = lax.all_gather(a_live, ('pair', 'odd', 'core'), axis=0, tiled=False)  11.5 us
    all_gather x1, waiting for transfers between devices, per_device(): lax.all_gather(jnp.where(lax.axis_index('odd') == core, column, beside),...  10.5 us
    ppermute x1, starting transfers between devices, per_device(): other = lax.ppermute(column, 'core', [(0, 1), (1, 0)])  8.79 us
    ppermute x1, waiting for transfers between devices, per_device(): beside = lax.ppermute(column, ('odd', 'core'), [(0, 2), (3, 1)])  5.81 us
    unnamed x4, local copies, waits for them, and re-layouts  4.97 us
  transfers between devices with their start and end apart: 5, of which 4 were waited for; matrix products, arithmetic and copies ran while one was open for 4% of the time, Pallas kernels for 3%

profile of v5, /device:TPU:1, one launch (start us, length us, event | category | flops | bytes accessed | tf_op | source)
XLA Modules:
  0.0 138.4 jit_solution(8204978628843303724)
XLA Ops:
  6.5 0.7 broadcast_compare_fusion
  7.3 2.0 %broadcast_select_fusion = bf16[16,2,64,128]{3,2,1,0:T(8,128)(2,1)} fusion(bf16[16,2,64,128]{3,2,1,0:T(8,128)(2,1)} %param.4, pred[16,2]{1,0:T(8,128)(4,1)S(1)} %copy.14), kind=kLoop, calls=%fused_computation | loop fusion | flops 262144 | bytes 1048608 | tf_op jit(solution)/shard_map/jit(_where)/select_n | solution.py:122
  9.4 0.7 broadcast_compare_fusion.1
  10.2 1.1 broadcast_select_fusion.1
  11.3 0.2 reshape.28
  11.6 2.0 %copy.13 = bf16[16,64,2,64]{3,2,1,0:T(2,128)(2,1)S(1)} copy(bf16[16,64,2,64]{1,2,3,0:T(2,128)(2,1)S(1)} %bitcast.16) | data formatting | bytes 524288 | tf_op jit(solution)/shard_map/transpose | solution.py:115
  13.6 0.2 reshape.29
  13.8 8.8 %collective-permute-start = (bf16[16,64,128]{2,1,0:T(8,128)(2,1)S(1)}, bf16[16,64,128]{2,1,0:T(8,128)(2,1)S(1)}, u32[]{:S(2)}, u32[]{:S(2)}) collective-permute-start(bf16[16,64,128]{2,1,0:T(8,128)(2,1)S(1)} %reshape.29), channel_id=1, source_target_pairs={{0,4},{4,0},{1,5},{5,1},{2,6},{6,2},{3,7},{7,3},{8,12},{12,8},{9,1... | collective-permute-start | bytes 786440 | tf_op jit(solution)/shard_map/ppermute | solution.py:135
  22.7 1.1 collective-permute-done
  23.8 1.3 collective-permute-start.1
  25.1 5.8 %collective-permute-done.1 = bf16[16,64,128]{2,1,0:T(8,128)(2,1)S(1)} collective-permute-done((bf16[16,64,128]{2,1,0:T(8,128)(2,1)S(1)}, bf16[16,64,128]{2,1,0:T(8,128)(2,1)S(1)}, u32[]{:S(2)}, u32[]{:S(2)}) %collective-permute-start.1) | collective-permute-done | bytes 262176 | tf_op jit(solution)/shard_map/ppermute | solution.py:137
  30.9 0.7 broadcast_select_fusion.3
  32.0 31.3 %all_to_all.20 = bf16[8,2,2,2,64,128]{5,4,3,2,1,0:T(8,128)(2,1)S(1)} all-to-all(bf16[8,2,2,2,64,128]{5,4,3,2,1,0:T(8,128)(2,1)S(1)} %broadcast_in_dim.25), channel_id=1, replica_groups=mesh['row'=8,'pair'=4,'odd'=2,'core'=2,'rep'=4] {'row'}, dimensions={0} | all-to-all | bytes 2097152 | tf_op jit(solution)/shard_map/all_to_all | solution.py:129
  63.2 11.5 %all-gather.7.cloned.1.call-done = bf16[256,2,64,128]{3,2,1,0:T(8,128)(2,1)} async-done(((bf16[16,2,64,128]{3,2,1,0:T(8,128)(2,1)}), bf16[256,2,64,128]{3,2,1,0:T(8,128)(2,1)}) %all-gather.7.cloned.1.call-update) | async-done | bytes 8388624 | tf_op jit(solution)/shard_map/all_gather | solution.py:123
  74.8 3.4 %copy-done = bf16[256,2,64,128]{3,2,1,0:T(8,128)(2,1)S(1)} copy-done((bf16[256,2,64,128]{3,2,1,0:T(8,128)(2,1)S(1)}, bf16[256,2,64,128]{3,2,1,0:T(8,128)(2,1)}, u32[]{:S(2)}) %copy-start) | copy-done | bytes 8388632
  78.1 3.4 %product_terms.1 = f32[16,2,64,128]{3,2,1,0:T(8,128)S(1)} custom-call(bf16[16,16,2,64,128]{4,3,2,1,0:T(8,128)(2,1)S(1)} %bitcast.11, bf16[16,2,2,64,128]{4,3,2,1,0:T(8,128)(2,1)S(1)} %bitcast.12), custom_call_target="tpu_custom_call" | custom-call | tf_op jit(solution)/shard_map/product_terms/pallas_call | solution.py:48
  81.6 18.5 %all_to_all.21 = f32[16,2,64,128]{3,2,1,0:T(8,128)S(1)} all-to-all(f32[16,2,64,128]{3,2,1,0:T(8,128)S(1)} %product_terms.1), channel_id=1, replica_groups=mesh['row'=8,'pair'=4,'odd'=2,'core'=2,'rep'=4] {'rep'}, dimensions={0} | all-to-all | bytes 2097152 | tf_op jit(solution)/shard_map/all_to_all | solution.py:143
  100.1 0.8 shard_map.46
  101.0 3.5 %all-to-all-start.2 = ((bf16[4,4,2,64,128]{4,3,2,1,0:T(8,128)(2,1)}), bf16[4,4,2,64,128]{4,3,2,1,0:T(8,128)(2,1)S(1)}, u32[]{:S(2)}, u32[]{:S(2)}) async-start(bf16[4,4,2,64,128]{4,3,2,1,0:T(8,128)(2,1)} %shard_map.46), calls=%async_computation.2 | async-start | bytes 1048576 | tf_op jit(solution)/shard_map/all_to_all | solution.py:150
  104.5 10.5 %all-gather.5.cloned.1.call-done = bf16[128,64,128]{2,1,0:T(8,128)(2,1)} async-done(((bf16[16,64,128]{2,1,0:T(8,128)(2,1)}), bf16[128,64,128]{2,1,0:T(8,128)(2,1)}) %all-gather.5.cloned.1.call-update) | async-done | bytes 2097168 | tf_op jit(solution)/shard_map/all_gather | solution.py:138
  114.9 1.6 %copy-done.1 = bf16[128,64,128]{2,1,0:T(8,128)(2,1)S(1)} copy-done((bf16[128,64,128]{2,1,0:T(8,128)(2,1)S(1)}, bf16[128,64,128]{2,1,0:T(8,128)(2,1)}, u32[]{:S(2)}) %copy-start.1) | copy-done | bytes 2097176
  116.5 0.8 shard_map.47
  117.3 13.6 %all_to_all.22.in_ref = bf16[8,2,64,128]{3,2,1,0:T(8,128)(2,1)S(1)} all-to-all(bf16[8,2,64,128]{3,2,1,0:T(8,128)(2,1)S(1)} %shard_map.47), channel_id=1, replica_groups=mesh['row'=8,'pair'=4,'odd'=2,'core'=2,'rep'=4] {'row'}, dimensions={0} | all-to-all | bytes 524288 | tf_op jit(solution)/shard_map/all_to_all | solution.py:157
  130.9 0.7 shard_map.48
  (13 shorter events, 0.6 us)
Async XLA Ops:
  6.5 68.2 %all-gather.7.cloned.1.call-start = ((), (), s32[]{:S(2)}) async-start(), calls=%async_computation.5 | async-start | bytes 8912896 | tf_op jit(solution)/shard_map/all_gather | solution.py:123
  9.3 105.6 %all-gather.5.cloned.1.call-start = ((), (), s32[]{:S(2)}) async-start(), calls=%async_computation.4 | async-start | bytes 2359296 | tf_op jit(solution)/shard_map/all_gather | solution.py:138
  13.8 9.9 %collective-permute-start = (bf16[16,64,128]{2,1,0:T(8,128)(2,1)S(1)}, bf16[16,64,128]{2,1,0:T(8,128)(2,1)S(1)}, u32[]{:S(2)}, u32[]{:S(2)}) collective-permute-start(bf16[16,64,128]{2,1,0:T(8,128)(2,1)S(1)} %reshape.29), channel_id=1, source_target_pairs={{0,4},{4,0},{1,5},{5,1},{2,6},{6,2},{3,7},{7,3},{8,12},{12,8},{9,1... | collective-permute-start | bytes 786440 | tf_op jit(solution)/shard_map/ppermute | solution.py:135
  23.8 7.1 %collective-permute-start.1 = (bf16[16,64,128]{2,1,0:T(8,128)(2,1)S(1)}, bf16[16,64,128]{2,1,0:T(8,128)(2,1)S(1)}, u32[]{:S(2)}, u32[]{:S(2)}) collective-permute-start(bf16[16,64,128]{2,1,0:T(8,128)(2,1)S(1)} %broadcast_select_fusion.2), channel_id=1, source_target_pairs={{0,8},{12,4},{1,9},{13,5},{2,10},{14,6},{3,11},{15,7},{16,24},{28,... | collective-permute-start | bytes 786440 | tf_op jit(solution)/shard_map/ppermute | solution.py:137
  74.8 3.4 %copy-start = (bf16[256,2,64,128]{3,2,1,0:T(8,128)(2,1)S(1)}, bf16[256,2,64,128]{3,2,1,0:T(8,128)(2,1)}, u32[]{:S(2)}) copy-start(bf16[256,2,64,128]{3,2,1,0:T(8,128)(2,1)} %all-gather.7.cloned.1.call-done) | copy-start | bytes 25165828
  101.0 13.9 %all-to-all-start.2 = ((bf16[4,4,2,64,128]{4,3,2,1,0:T(8,128)(2,1)}), bf16[4,4,2,64,128]{4,3,2,1,0:T(8,128)(2,1)S(1)}, u32[]{:S(2)}, u32[]{:S(2)}) async-start(bf16[4,4,2,64,128]{4,3,2,1,0:T(8,128)(2,1)} %shard_map.46), calls=%async_computation.2 | async-start | bytes 1048576 | tf_op jit(solution)/shard_map/all_to_all | solution.py:150
  114.9 1.6 %copy-start.1 = (bf16[128,64,128]{2,1,0:T(8,128)(2,1)S(1)}, bf16[128,64,128]{2,1,0:T(8,128)(2,1)}, u32[]{:S(2)}) copy-start(bf16[128,64,128]{2,1,0:T(8,128)(2,1)} %all-gather.5.cloned.1.call-done) | copy-start | bytes 6291460
Sparse Core Ops, SparseCore 0:
  9.5 65.2 all-gather.6
  76.9 37.9 all-gather.4
